TPU v7x, 256 devices: a whole 4x4x8 slice. The times are simulated.
256 devices in a mesh: expert: 32 (over z, y), seq: 4 (over x), dp: 2 (over core).
Axes of the slice: x: 4, y: 4, z: 8, core: 2. Of those that a mesh axis runs over, the one named last changes fastest.
Arguments:
- hidden_in: bfloat16 [32768, 2048], P(('expert', 'seq', 'dp')), may hold values from -20 to 20
- norm_gain: float32 [2048], replicated, may hold values from 0.5 to 1.5
- router_weight: bfloat16 [2048, 64], replicated, may hold values from -0.125 to 0.125
- routes: int32 [32768, 6], P(('expert', 'seq', 'dp')), may hold values from 0 to 63, all different within a row; in each aligned block of 128 rows (0 to 127, 128 to 255, ...) at most 13 rows name the same one
- w_gate: bfloat16 [64, 2048, 1408], P(('expert', 'dp'), 'seq'), may hold values from -0.125 to 0.125
- w_up: bfloat16 [64, 2048, 1408], P(('expert', 'dp'), 'seq'), may hold values from -0.125 to 0.125
- w_down: bfloat16 [64, 1408, 2048], P(('expert', 'dp'), 'seq'), may hold values from -0.15625 to 0.15625
- cached_layers: bfloat16 [3, 32768, 2048], P(None, ('expert', 'seq', 'dp')), may hold values from -40 to 40
- student_hidden: bfloat16 [32768, 2048], P(('expert', 'seq', 'dp')), may hold values from -24 to 24
- prediction: bfloat16 [32768, 1024], P(('expert', 'seq', 'dp')), may hold values from -6 to 6
Outputs:
- targets: bfloat16 [32768, 2048], P(('expert', 'seq', 'dp'))
- head_grad: float32 [2048, 1024], P(('expert', 'seq', 'dp'))
Inputs may be any that keep to these rules, and one draw needn't show every extreme that they name: `routes`: each row names 6 different experts. Among the 128 rows of one device no expert is named more than 13 times, a bound that some block reaches.
All inputs are finite; a program needn't handle non-finite values.
Results may differ from a plain program's by a relative error of at most 0.0025.
The roundings to bfloat16 on the way count: a program that leaves them out, or rounds other values in their place, can miss the bound.
Values may be sent and summed in bfloat16 or wider, within the bound.
A program may use at most 128 MiB of HBM per device.

v0:
```python
import math

import jax
import jax.numpy as jnp
from jax import lax
from jax.sharding import PartitionSpec as P


def body(
    hidden_in,
    norm_gain,
    router_weight,
    routes,
    w_gate,
    w_up,
    w_down,
    cached_layers,
    student_hidden,
    prediction,
):
    tok_rows, width = hidden_in.shape
    n_experts = router_weight.shape[1]
    top_k = routes.shape[1]
    capacity = 9 * tok_rows * top_k // (8 * n_experts)
    all_devices = lax.axis_size(("expert", "seq", "dp"))
    token_total = tok_rows * all_devices
    cached32 = cached_layers.astype(jnp.float32)
    cached_sums = jnp.sum(cached32, axis=1)
    cached_squares = jnp.sum(cached32 * cached32, axis=1)
    hidden32 = hidden_in.astype(jnp.float32)
    normed = (
        hidden32
        * lax.rsqrt(jnp.mean(hidden32 * hidden32, axis=-1, keepdims=True) + 1e-06)
        * norm_gain
    ).astype(jnp.bfloat16)
    logits = jnp.dot(normed, router_weight, preferred_element_type=jnp.float32)
    picked = routes[:, :, None] == jnp.arange(n_experts, dtype=jnp.int32)[None, None, :]
    chosen = jnp.sum(jnp.where(picked, logits[:, None, :], jnp.zeros((), jnp.float32)), axis=-1)
    affinity = jax.nn.sigmoid(chosen)
    gate_share = affinity / jnp.sum(affinity, axis=-1, keepdims=True)
    flags = picked.reshape(tok_rows * top_k, n_experts).astype(jnp.int32)
    running = jnp.cumsum(flags, axis=0)
    slot_index = jnp.sum(running * flags, axis=-1) - 1
    target_row = routes.reshape(-1) * capacity + slot_index
    owners = jnp.arange(tok_rows * top_k, dtype=jnp.int32) // top_k
    source_row = jnp.full((n_experts * capacity,), tok_rows, jnp.int32).at[target_row].set(owners)
    padded = jnp.concatenate([normed, jnp.zeros((1, width), jnp.bfloat16)], axis=0)
    outgoing = jnp.take(padded, source_row, axis=0).reshape(n_experts, capacity, width)
    incoming = lax.all_to_all(outgoing, ("expert", "dp"), split_axis=0, concat_axis=0, tiled=True)
    expert_rows = incoming.reshape(n_experts * capacity, width)
    gate_rows = w_gate[0]
    up_rows = w_up[0]
    columns = expert_rows
    gate_acc = jnp.dot(
        columns,
        lax.all_gather(gate_rows, "seq", axis=0, tiled=True),
        preferred_element_type=jnp.float32,
    )
    up_acc = jnp.dot(
        columns,
        lax.all_gather(up_rows, "seq", axis=0, tiled=True),
        preferred_element_type=jnp.float32,
    )
    activation = (jax.nn.silu(gate_acc) * up_acc).astype(jnp.bfloat16)
    columns = activation
    expert_out = jnp.dot(
        columns,
        lax.all_gather(w_down[0], "seq", axis=0, tiled=True),
        preferred_element_type=jnp.float32,
    ).astype(jnp.bfloat16)
    returned = lax.all_to_all(
        expert_out.reshape(n_experts, capacity, width),
        ("expert", "dp"),
        split_axis=0,
        concat_axis=0,
        tiled=True,
    )
    returned = returned.reshape(n_experts * capacity, width)
    routed = (
        jnp.take(returned, target_row, axis=0).reshape(tok_rows, top_k, width).astype(jnp.float32)
    )
    mixture = jnp.einsum("tk,tkd->td", gate_share, routed)
    layer_out = hidden32 + mixture
    out_sums = jnp.sum(layer_out, axis=0)
    out_squares = jnp.sum(layer_out * layer_out, axis=0)
    layer_sums, layer_squares = lax.psum(
        (
            jnp.concatenate([cached_sums, out_sums[None, :]], axis=0),
            jnp.concatenate([cached_squares, out_squares[None, :]], axis=0),
        ),
        ("expert", "seq", "dp"),
    )
    means = layer_sums / token_total
    variance = layer_squares / token_total - means * means
    inverse = lax.rsqrt(variance + 1e-05)
    stacked = jnp.concatenate([cached32, layer_out[None, :, :]], axis=0)
    targets = jnp.mean((stacked - means[:, None, :]) * inverse[:, None, :], axis=0).astype(
        jnp.bfloat16
    )
    window = prediction.shape[1]
    scale = 1.0 / math.sqrt(token_total)
    residual = (
        (prediction.astype(jnp.float32) - targets[:, :window].astype(jnp.float32)) * scale
    ).astype(jnp.bfloat16)
    columns = student_hidden
    head_grad = lax.psum_scatter(
        lax.dot_general(
            columns, residual, (((0,), (0,)), ((), ())), preferred_element_type=jnp.float32
        ),
        ("expert", "seq", "dp"),
        scatter_dimension=0,
        tiled=True,
    )
    return (targets, head_grad)


def solution(mesh):
    placed = (
        P(("expert", "seq", "dp"), None),
        P(),
        P(),
        P(("expert", "seq", "dp"), None),
        P(("expert", "dp"), "seq", None),
        P(("expert", "dp"), "seq", None),
        P(("expert", "dp"), "seq", None),
        P(None, ("expert", "seq", "dp"), None),
        P(("expert", "seq", "dp"), None),
        P(("expert", "seq", "dp"), None),
    )
    return jax.shard_map(
        body,
        mesh=mesh,
        in_specs=placed,
        out_specs=(P(("expert", "seq", "dp"), None), P(("expert", "seq", "dp"), None)),
        check_vma=False,
    )
```

profile of v0, /device:TPU:1, one launch (start us, length us, event | category | flops | bytes accessed | tf_op | source)
XLA Modules:
  0.0 1897.9 jit_solution(7934694461439148208)
XLA Ops:
  10.1 1.8 reduce-window.6
  12.4 3.4 scatter_custom_fusion
  16.3 4.9 gather_fusion
  21.2 4.9 gather.13
  26.3 3.0 broadcast_select_fusion
  29.3 107.7 %all_to_all.10 = bf16[64,13,2048]{2,1,0:T(8,128)(2,1)} all-to-all(bf16[64,13,2048]{2,1,0:T(8,128)(2,1)S(1)} %broadcast_select_fusion), channel_id=1, replica_groups=mesh['expert'=32,'seq'=4,'dp'=2] {'expert','dp'}, dimensions={0} | all-to-all | bytes 6815744 | tf_op jit(solution)/shard_map/all_to_all | solution.py:49
  137.0 5.0 reshape.109
  142.0 10.2 fusion.2
  152.2 57.9 %all-gather.7.cloned.1.call-done = bf16[1,2048,1408]{2,1,0:T(8,128)(2,1)} async-done(((bf16[1,512,1408]{2,1,0:T(8,128)(2,1)}), bf16[1,2048,1408]{2,1,0:T(8,128)(2,1)}) %all-gather.7.cloned.1.call-update) | async-done | bytes 5767184 | tf_op jit(solution)/shard_map/all_gather | solution.py:56
  210.2 17.9 fusion.13
  228.1 4.9 reshape.110
  233.0 11.2 all-to-all-start.1
  245.8 92.9 %all-to-all-done.1 = bf16[64,13,2048]{2,1,0:T(8,128)(2,1)} async-done(((bf16[64,13,2048]{2,1,0:T(8,128)(2,1)}), bf16[64,13,2048]{2,1,0:T(8,128)(2,1)}, u32[]{:S(2)}, u32[]{:S(2)}) %all-to-all-start.1) | async-done | bytes 3407904 | tf_op jit(solution)/shard_map/all_to_all | solution.py:71
  338.7 5.0 reshape.111
  343.7 9.5 gather_fusion.1
  353.1 6.3 gather.15
  359.4 3.5 fusion.10
  362.9 1.5 fusion.22
  365.1 2.0 convert_element_type.33
  367.2 233.6 %all-reduce.4.cloned.1.call-done = (f32[4,2048]{1,0:T(4,128)}, f32[4,2048]{1,0:T(4,128)}) async-done(((f32[4,2048]{1,0:T(4,128)}, f32[4,2048]{1,0:T(4,128)}), (f32[4,2048]{1,0:T(4,128)}, f32[4,2048]{1,0:T(4,128)})) %all-reduce.4.cloned.1.call-update) | async-done | bytes 65552 | tf_op jit(solution)/shard_map/psum | solution.py:86
  601.5 2.6 fusion.9
  604.2 4.5 convolution_bitcast_fusion
  608.7 9.3 copy.44
  618.0 1273.3 %reduce-scatter.4.cloned.1.call-done = f32[8,1024]{1,0:T(8,128)} async-done(((f32[2048,1024]{1,0:T(8,128)}), f32[8,1024]{1,0:T(8,128)}) %reduce-scatter.4.cloned.1.call-update) | async-done | bytes 32784
  (65 shorter events, 6.9 us)
Async XLA Ops:
  7.2 597.0 %copy-start = (bf16[128,2048]{1,0:T(8,128)(2,1)S(1)}, bf16[128,2048]{1,0:T(8,128)(2,1)}, u32[]{:S(2)}) copy-start(bf16[128,2048]{1,0:T(8,128)(2,1)} %param.18) | copy-start | bytes 1572868
  7.2 2.3 copy-start.7
  7.2 8.6 copy-start.2
  7.2 8.8 copy-start.8
  7.2 134.8 %all-gather.9.cloned.1.call-start = ((), (), s32[]{:S(2)}) async-start(), calls=%async_computation.4 | async-start | bytes 7208960 | tf_op jit(solution)/shard_map/all_gather | solution.py:61
  7.9 144.3 %all-gather.11.cloned.1.call-start = ((), (), s32[]{:S(2)}) async-start(), calls=%async_computation.5 | async-start | bytes 7208960 | tf_op jit(solution)/shard_map/all_gather | solution.py:68
  8.7 201.5 %all-gather.7.cloned.1.call-start = ((), (), s32[]{:S(2)}) async-start(), calls=%async_computation.3 | async-start | bytes 7208960 | tf_op jit(solution)/shard_map/all_gather | solution.py:56
  233.0 11.4 copy-start.6
  233.0 12.2 copy-start.1
  233.0 105.7 %all-to-all-start.1 = ((bf16[64,13,2048]{2,1,0:T(8,128)(2,1)}), bf16[64,13,2048]{2,1,0:T(8,128)(2,1)}, u32[]{:S(2)}, u32[]{:S(2)}) async-start(bf16[64,13,2048]{2,1,0:T(8,128)(2,1)} %reshape.110), calls=%async_computation.1 | async-start | bytes 8388608 | tf_op jit(solution)/shard_map/all_to_all | solution.py:71
  244.3 356.4 %all-reduce.4.cloned.1.call-start = ((), (), s32[]{:S(2)}) async-start(), calls=%async_computation.7 | async-start | bytes 131072 | tf_op jit(solution)/shard_map/psum | solution.py:86
  364.4 237.1 %copy-start.3 = (f32[1,128,2048]{2,1,0:T(8,128)S(1)}, f32[1,128,2048]{2,1,0:T(8,128)}, u32[]{:S(2)}) copy-start(f32[1,128,2048]{2,1,0:T(8,128)} %get-tuple-element.18) | copy-start | bytes 3145732
  365.1 1526.3 %reduce-scatter.4.cloned.1.call-start = ((), (), s32[]{:S(2)}) async-start(), calls=%async_computation.6 | async-start | bytes 8421376
  367.2 237.0 %copy-start.5 = (bf16[128,1024]{1,0:T(8,128)(2,1)S(1)}, bf16[128,1024]{1,0:T(8,128)(2,1)}, u32[]{:S(2)}) copy-start(bf16[128,1024]{1,0:T(8,128)(2,1)} %param.19) | copy-start | bytes 786436
  604.2 4.5 copy-start.4
Sparse Core Ops, SparseCore 0:
  9.9 67.6 all-gather.8
  79.3 64.4 all-gather.10
  145.7 64.4 all-gather.6
  365.2 235.4 all-reduce.3
  618.1 1273.1 reduce-scatter.3
where the time goes:
time: 1900 us
  waiting for transfers between devices  1660 us (87%)
  blocking collectives  108 us (6%)
  local copies, waits for them, and re-layouts  54.7 us (3%)
  matrix products  36.5 us (2%)
    unnamed x6, waiting for transfers between devices  1280 us
    psum x1, waiting for transfers between devices, body(): lax.psum((jnp.concatenate([cached_sums, out_sums[None, :]], axis=0), jnp....  234 us
    all_to_all x1, blocking collectives, body(): lax.all_to_all(outgoing, ('expert', 'dp'), split_axis=0, concat_axis=0, t...  108 us
    all_to_all x1, waiting for transfers between devices, body(): lax.all_to_all(expert_out.reshape(n_experts, capacity, width), ('expert',...  92.9 us
    all_gather x1, waiting for transfers between devices, body(): lax.all_gather(gate_rows, 'seq', axis=0, tiled=True)  57.9 us
  transfers between devices with their start and end apart: 6, of which 4 were waited for; matrix products, arithmetic and copies ran while one was open for 2% of the time, Pallas kernels for 0%

commit v1 on v0

v1 whole, which is shorter than its diff:
```python
import functools
import math

import jax
import jax.numpy as jnp
from jax import lax
from jax.experimental import pallas as pl
from jax.experimental.pallas import tpu as pltpu
from jax.sharding import PartitionSpec as P

MESH = pl.DeviceIdType.MESH
F32, BF16 = jnp.float32, jnp.bfloat16
NY = 4


def wheel():
    e, x, c = lax.axis_index("expert"), lax.axis_index("seq"), lax.axis_index("dp")
    nz = lax.axis_size("expert") // NY
    z, y = e // NY, lax.rem(e, NY)

    def to(z_, y_, x_, c_):
        return {"expert": z_ * NY + y_, "seq": x_, "dp": c_}

    return {
        "c": (c, 2, lambda d: to(z, y, x, lax.rem(c + d, 2))),
        "x": (x, lax.axis_size("seq"), lambda d: to(z, y, lax.rem(x + d, lax.axis_size("seq")), c)),
        "y": (y, NY, lambda d: to(z, lax.rem(y + d, NY), x, c)),
        "z": (z, nz, lambda d: to(lax.rem(z + d, nz), y, x, c)),
    }


def start_all(axis, source, target, send, recv):
    _, n, device = axis
    copies = []
    for d in range(1, n):
        copy = pltpu.make_async_remote_copy(
            src_ref=source(d),
            dst_ref=target(d),
            send_sem=send.at[d - 1],
            recv_sem=recv.at[d - 1],
            device_id=device(d),
            device_id_type=MESH,
        )
        copy.start()
        copies.append(copy)
    return copies


def wait_all(copies):
    for copy in copies:
        copy.wait()


def fold(row_list):
    w = row_list[0].shape[1] // 4
    return jnp.concatenate([r[:, i * w : (i + 1) * w] for r in row_list for i in range(4)], axis=0)


def unfold(block, row):
    return jnp.concatenate([block[4 * row + i : 4 * row + i + 1, :] for i in range(4)], axis=1)


def column_sums(values):
    return [jnp.sum(values, axis=0, keepdims=True), jnp.sum(values * values, axis=0, keepdims=True)]


def tail_kernel(
    total_tokens,
    back_ref,
    mix_ref,
    hidden_ref,
    cached_ref,
    prediction_ref,
    student_ref,
    targets_ref,
    grad_ref,
    layer_out,
    stat_own,
    stat_c,
    stat_x,
    stat_y,
    stat_z,
    students,
    residuals,
    partial,
    from_c,
    from_y,
    from_z,
    sem_st,
    sem_s,
    sem_x,
    sem_c,
    sem_y,
    sem_z,
):
    axes = wheel()
    tok, width = hidden_ref.shape
    window = prediction_ref.shape[1]
    x = axes["x"][0]
    c = axes["c"][0]

    barrier = pltpu.get_barrier_semaphore()
    greeted = 0
    for name in "cxyz":
        _, n, device = axes[name]
        for d in range(1, n):
            pl.semaphore_signal(barrier, inc=1, device_id=device(d), device_id_type=MESH)
            greeted += 1
    pl.semaphore_wait(barrier, greeted)

    nx = axes["x"][1]
    students_out = start_all(
        axes["x"],
        lambda d: student_ref.at[lax.rem(x + d, nx)],
        lambda d: students.at[d],
        sem_st.at[0],
        sem_st.at[1],
    )

    stats = []
    for layer in range(3):
        stats += column_sums(cached_ref[layer].astype(F32))
    cut = 512
    for j in range(width // cut):
        cols = slice(j * cut, (j + 1) * cut)
        both = jnp.dot(mix_ref[...], back_ref[:, cols], preferred_element_type=F32)
        layer_out[:, cols] = hidden_ref[:, cols].astype(F32) + (both[:tok] + both[tok:])
    stats += column_sums(layer_out[...])
    stat_own[0] = fold(stats)
    for i, (name, slots) in enumerate((("c", stat_c), ("x", stat_x), ("y", stat_y), ("z", stat_z))):
        copies = start_all(
            axes[name],
            lambda d, i=i: stat_own.at[i],
            lambda d, slots=slots: slots.at[d - 1],
            sem_s.at[i, 0],
            sem_s.at[i, 1],
        )
        for copy in copies:
            copy.wait_recv()
        total = stat_own[i]
        for d in range(1, axes[name][1]):
            total = total + slots[d - 1]
        stat_own[i + 1] = total
        for copy in copies:
            copy.wait_send()
    total = stat_own[4]
    for j in range(width // cut):
        cols = slice(j * cut, (j + 1) * cut)
        summed = jnp.zeros((tok, cut), F32)
        for layer in range(4):
            mean = total[8 * layer + j : 8 * layer + j + 1, :] / total_tokens
            square = total[8 * layer + 4 + j : 8 * layer + 5 + j, :] / total_tokens
            inverse = lax.rsqrt(square - mean * mean + 1e-5)
            values = cached_ref[layer, :, cols].astype(F32) if layer < 3 else layer_out[:, cols]
            summed = summed + (values - mean) * inverse
        targets = (summed * 0.25).astype(BF16)
        targets_ref[:, cols] = targets
        if (j + 1) * cut <= window:
            scale = 1.0 / math.sqrt(total_tokens)
            residuals[0, :, cols] = (
                (prediction_ref[:, cols].astype(F32) - targets.astype(F32)) * scale
            ).astype(BF16)

    copies = start_all(
        axes["x"],
        lambda d: residuals.at[0],
        lambda d: residuals.at[d],
        sem_x.at[0],
        sem_x.at[1],
    )
    for copy in students_out:
        copy.wait()
    students[0] = student_ref[x]
    rows = partial.shape[0]
    half = rows // 2
    for d in range(nx):
        if d:
            copies[d - 1].wait_recv()

        def add(i, _):
            at = pl.ds(pl.multiple_of(i * 128, 128), 128)
            product = jnp.dot(students[d, at, :], residuals[d], preferred_element_type=F32)
            partial[at, :] = product if d == 0 else partial[at, :] + product
            return _

        lax.fori_loop(0, rows // 128, add, 0)
    for copy in copies:
        copy.wait_send()
    other = pl.ds(pl.multiple_of((1 - c) * half, half), half)
    mine = pl.ds(pl.multiple_of(c * half, half), half)
    wait_all(
        start_all(
            axes["c"],
            lambda d: partial.at[other],
            lambda d: from_c,
            sem_c.at[0],
            sem_c.at[1],
        )
    )
    from_c[...] = from_c[...] + partial[mine, :]
    y, ny, _ = axes["y"]
    part = half // ny

    def y_rows(d):
        return pl.ds(pl.multiple_of(lax.rem(y + d, ny) * part, part), part)

    wait_all(
        start_all(
            axes["y"],
            lambda d: from_c.at[y_rows(d)],
            lambda d: from_y.at[d],
            sem_y.at[0],
            sem_y.at[1],
        )
    )
    total = from_c[y_rows(0), :]
    for d in range(1, ny):
        total = total + from_y[d]
    from_y[0] = total
    z, nz, _ = axes["z"]
    least = part // nz

    def z_rows(d):
        return pl.ds(pl.multiple_of(lax.rem(z + d, nz) * least, least), least)

    wait_all(
        start_all(
            axes["z"],
            lambda d: from_y.at[0, z_rows(d)],
            lambda d: from_z.at[d],
            sem_z.at[0],
            sem_z.at[1],
        )
    )
    total = from_y[0, z_rows(0), :]
    for d in range(1, nz):
        total = total + from_z[d]
    grad_ref[...] = total


def tail(total_tokens, back, mix, hidden_in, cached, prediction, student):
    tok, width = hidden_in.shape
    window = prediction.shape[1]
    nx, ny, nz = lax.axis_size("seq"), NY, lax.axis_size("expert") // NY
    rows = width // nx
    vmem = pl.BlockSpec(memory_space=pltpu.VMEM)
    dma = pltpu.SemaphoreType.DMA
    stat = (32, width // 4)
    return pl.pallas_call(
        functools.partial(tail_kernel, total_tokens),
        out_shape=(
            jax.ShapeDtypeStruct((tok, width), BF16),
            jax.ShapeDtypeStruct((rows // (2 * ny * nz), window), F32),
        ),
        in_specs=[vmem] * 6,
        out_specs=(vmem, vmem),
        scratch_shapes=[
            pltpu.VMEM((tok, width), F32),
            pltpu.VMEM((5, *stat), F32),
            pltpu.VMEM((1, *stat), F32),
            pltpu.VMEM((nx - 1, *stat), F32),
            pltpu.VMEM((ny - 1, *stat), F32),
            pltpu.VMEM((nz - 1, *stat), F32),
            pltpu.VMEM((nx, rows, tok), BF16),
            pltpu.VMEM((nx, tok, window), BF16),
            pltpu.VMEM((rows, window), F32),
            pltpu.VMEM((rows // 2, window), F32),
            pltpu.VMEM((ny, rows // (2 * ny), window), F32),
            pltpu.VMEM((nz, rows // (2 * ny * nz), window), F32),
            dma((2, nx - 1)),
            dma((4, 2, 7)),
            dma((2, nx - 1)),
            dma((2, 1)),
            dma((2, ny - 1)),
            dma((2, nz - 1)),
        ],
        compiler_params=pltpu.CompilerParams(
            collective_id=1, has_side_effects=True, vmem_limit_bytes=40 * 2**20
        ),
    )(back, mix, hidden_in, cached, prediction, student)


SLOTS = 16


def body(
    hidden_in,
    norm_gain,
    router_weight,
    routes,
    w_gate,
    w_up,
    w_down,
    cached_layers,
    student_hidden,
    prediction,
):
    tok, width = hidden_in.shape
    n_experts = router_weight.shape[1]
    nx, nz = lax.axis_size("seq"), lax.axis_size("expert") // NY
    total_tokens = tok * lax.axis_size(("expert", "seq", "dp"))
    hidden32 = hidden_in.astype(F32)
    normed = (
        hidden32
        * lax.rsqrt(jnp.mean(hidden32 * hidden32, axis=-1, keepdims=True) + 1e-06)
        * norm_gain
    ).astype(BF16)
    logits = jnp.dot(normed, router_weight, preferred_element_type=F32)
    picked = jnp.any(routes[:, :, None] == jnp.arange(n_experts, dtype=jnp.int32), axis=1)
    earlier = jnp.tril(jnp.ones((tok, tok), BF16), -1)
    place = jnp.dot(earlier, picked.astype(BF16), preferred_element_type=F32)
    affinity = jnp.where(picked, jax.nn.sigmoid(logits), 0.0)
    share = affinity / jnp.sum(affinity, axis=-1, keepdims=True)
    slots = jnp.arange(SLOTS, dtype=F32)
    where = picked[:, :, None] & (place[:, :, None] == slots)
    pick = where.reshape(tok, n_experts * SLOTS).astype(BF16)
    mix = jnp.where(where, share[:, :, None], 0.0).reshape(tok, n_experts * SLOTS)
    high = mix.astype(BF16)
    low = (mix - high.astype(F32)).astype(BF16)
    mix = jnp.concatenate([high, low], axis=0)
    outgoing = lax.dot_general(
        pick, normed, (((0,), (0,)), ((), ())), preferred_element_type=F32
    ).astype(BF16)

    def exchange(rows):
        return lax.all_to_all(
            rows.reshape(n_experts, SLOTS, width),
            ("expert", "dp"),
            split_axis=0,
            concat_axis=0,
            tiled=True,
        ).reshape(n_experts * SLOTS, width)

    rows = exchange(outgoing)
    gate_acc = jnp.dot(
        rows, lax.all_gather(w_gate[0], "seq", axis=0, tiled=True), preferred_element_type=F32
    )
    up_acc = jnp.dot(
        rows, lax.all_gather(w_up[0], "seq", axis=0, tiled=True), preferred_element_type=F32
    )
    activation = (jax.nn.silu(gate_acc) * up_acc).astype(BF16)
    expert_out = jnp.dot(
        activation,
        lax.all_gather(w_down[0], "seq", axis=0, tiled=True),
        preferred_element_type=F32,
    ).astype(BF16)
    back = exchange(expert_out)
    student = (
        student_hidden.T.reshape(nz, NY, nx, 2, width // (2 * nx * NY * nz), tok)
        .transpose(2, 3, 1, 0, 4, 5)
        .reshape(nx, width // nx, tok)
    )
    return tail(total_tokens, back, mix, hidden_in, cached_layers, prediction, student)


def solution(mesh):
    tokens = P(("expert", "seq", "dp"), None)
    weights = P(("expert", "dp"), "seq", None)
    return jax.shard_map(
        body,
        mesh=mesh,
        in_specs=(
            tokens,
            P(),
            P(),
            tokens,
            weights,
            weights,
            weights,
            P(None, ("expert", "seq", "dp"), None),
            tokens,
            tokens,
        ),
        out_specs=(tokens, tokens),
        check_vma=False,
    )
```

time: 1900 us -> 422 us (0.22)
  waiting for transfers between devices: 1660 us -> 260 us
  blocking collectives: 108 us -> 0 us
  Pallas kernels: 0 us -> 76.3 us
  local copies, waits for them, and re-layouts: 54.7 us -> 5.39 us
    unnamed x6 -> x3, waiting for transfers between devices: 1280 us -> 2.06 us
    psum x1 -> x0, waiting for transfers between devices: 234 us -> none  [body(): lax.psum((jnp.concatenate([cached_sums, out_sums[None, :]], axis=0), jnp....]
    all_to_all x1 -> x0, blocking collectives: 108 us -> none  [body(): lax.all_to_all(outgoing, ('expert', 'dp'), split_axis=0, concat_axis=0, t...]
    all_to_all x1 -> x2, waiting for transfers between devices: 92.9 us -> 185 us  [exchange(): lax.all_to_all(rows.reshape(n_experts, SLOTS, width), ('expert', 'dp'), s...]
    pallas_call x0 -> x1, Pallas kernels: none -> 76.3 us  [tail(): pl.pallas_call(functools.partial(tail_kernel, total_tokens), out_shape=(j...]
    gather x4 -> x0, local copies, waits for them, and re-layouts: 25.6 us -> none  [the longest x2 15.7 us: body(): jnp.take(returned, target_row, axis=0).reshape(tok_rows, top_k, width)]
  transfers between devices with their start and end apart: 6 -> 5, of which waited for: 4 -> 4; matrix products, arithmetic and copies ran while one was open for 2% -> 6% of each run, Pallas kernels for 0% -> 0%
where the time goes in v1:
time: 422 us; the launch traced here: 421 us
  waiting for transfers between devices  260 us (62%)
  Pallas kernels  76.3 us (18%)
  matrix products  37.3 us (9%)
  starting transfers between devices  24.5 us (6%)
  between operations  13.9 us (3%)
  local copies, waits for them, and re-layouts  5.39 us (1%)
    all_to_all x2, waiting for transfers between devices, exchange(): lax.all_to_all(rows.reshape(n_experts, SLOTS, width), ('expert', 'dp'), s...  185 us
    pallas_call x1, Pallas kernels, tail(): pl.pallas_call(functools.partial(tail_kernel, total_tokens), out_shape=(j...  76.3 us
    all_gather x1, waiting for transfers between devices, body(): lax.all_gather(w_up[0], 'seq', axis=0, tiled=True)  66.3 us
    all_to_all x2, starting transfers between devices, exchange(): lax.all_to_all(rows.reshape(n_experts, SLOTS, width), ('expert', 'dp'), s...  24.4 us
    dot_general x1, matrix products, body(): jnp.dot(activation, lax.all_gather(w_down[0], 'seq', axis=0, tiled=True),...  20.6 us
    dot_general x1, matrix products, body(): jnp.dot(rows, lax.all_gather(w_gate[0], 'seq', axis=0, tiled=True), prefe...  11.8 us
  transfers between devices with their start and end apart: 5, of which 4 were waited for; matrix products, arithmetic and copies ran while one was open for 6% of the time, Pallas kernels for 0%

profile of v1, /device:TPU:1, one launch (start us, length us, event | category | flops | bytes accessed | tf_op | source)
XLA Modules:
  0.0 421.5 jit_solution(7714247592989057387)
XLA Ops:
  7.2 0.7 all-gather.7.cloned.1.call-update
  8.0 0.7 all-gather.11.cloned.1.call-update
  8.7 0.7 fusion.23
  9.4 1.2 fusion.20
  10.7 1.4 fusion.35
  12.9 0.2 copy.24
  13.2 0.9 select_convert_fusion
  14.1 3.3 convolution_convert_fusion
  17.4 13.3 %all-to-all-start = ((bf16[64,16,2048]{2,1,0:T(8,128)(2,1)}), bf16[64,16,2048]{2,1,0:T(8,128)(2,1)}, u32[]{:S(2)}, u32[]{:S(2)}) async-start(bf16[64,16,2048]{2,1,0:T(8,128)(2,1)} %bitcast.36), calls=%async_computation | async-start | bytes 8388608 | tf_op jit(solution)/shard_map/all_to_all | solution.py:326
  30.8 0.7 all-gather.9.cloned.1.call-update
  31.5 93.7 %all-to-all-done = bf16[64,16,2048]{2,1,0:T(8,128)(2,1)} async-done(((bf16[64,16,2048]{2,1,0:T(8,128)(2,1)}), bf16[64,16,2048]{2,1,0:T(8,128)(2,1)}, u32[]{:S(2)}, u32[]{:S(2)}) %all-to-all-start) | async-done | bytes 4194336 | tf_op jit(solution)/shard_map/all_to_all | solution.py:326
  125.2 11.8 %fusion.4 = f32[1024,1408]{1,0:T(8,128)} fusion(bf16[1024,2048]{1,0:T(8,128)(2,1)} %bitcast.3, bf16[1,2048,1408]{2,1,0:T(8,128)(2,1)} %all-gather.7.cloned.1.call-done), kind=kOutput, calls=%fused_computation.4 | convolution fusion | flops 5905580032 | bytes 15728640 | tf_op jit(solution)/shard_map/dot_general | solution.py:335
  136.9 6.9 %all-gather.11.cloned.1.call-done = bf16[1,1408,2048]{2,1,0:T(8,128)(2,1)} async-done(((bf16[1,352,2048]{2,1,0:T(8,128)(2,1)}), bf16[1,1408,2048]{2,1,0:T(8,128)(2,1)}) %all-gather.11.cloned.1.call-update) | async-done | bytes 5767184 | tf_op jit(solution)/shard_map/all_gather | solution.py:344
  143.9 66.3 %all-gather.9.cloned.1.call-done = bf16[1,2048,1408]{2,1,0:T(8,128)(2,1)} async-done(((bf16[1,512,1408]{2,1,0:T(8,128)(2,1)}), bf16[1,2048,1408]{2,1,0:T(8,128)(2,1)}) %all-gather.9.cloned.1.call-update) | async-done | bytes 5767184 | tf_op jit(solution)/shard_map/all_gather | solution.py:339
  210.2 20.6 %fusion.10 = bf16[1024,2048]{1,0:T(8,128)(2,1)} fusion(bf16[1,1408,2048]{2,1,0:T(8,128)(2,1)} %all-gather.11.cloned.1.call-done, f32[1024,1408]{1,0:T(8,128)} %fusion.4, bf16[1024,2048]{1,0:T(8,128)(2,1)} %bitcast.3, bf16[1,2048,1408]{2,1,0:T(8,128)(2,1)} %all-gather.9.cloned.1.call-done), kind=kOutput, calls=%fused_computation.8 | convolution fusion | flops 11821907968 | bytes 25690112 | tf_op jit(solution)/shard_map/dot_general | solution.py:342
  230.8 11.1 %all-to-all-start.1 = ((bf16[64,16,2048]{2,1,0:T(8,128)(2,1)}), bf16[64,16,2048]{2,1,0:T(8,128)(2,1)}, u32[]{:S(2)}, u32[]{:S(2)}) async-start(bf16[64,16,2048]{2,1,0:T(8,128)(2,1)} %bitcast.37), calls=%async_computation.1 | async-start | bytes 8388608 | tf_op jit(solution)/shard_map/all_to_all | solution.py:326
  241.9 1.0 copy.26
  242.9 1.2 copy.27
  244.2 1.0 pad_maximum_fusion.mix_ref
  245.2 91.1 %all-to-all-done.1 = bf16[64,16,2048]{2,1,0:T(8,128)(2,1)} async-done(((bf16[64,16,2048]{2,1,0:T(8,128)(2,1)}), bf16[64,16,2048]{2,1,0:T(8,128)(2,1)}, u32[]{:S(2)}, u32[]{:S(2)}) %all-to-all-start.1) | async-done | bytes 4194336 | tf_op jit(solution)/shard_map/all_to_all | solution.py:326
  336.3 0.9 copy-done.3
  337.3 76.3 %shard_map.113 = (bf16[128,2048]{1,0:T(8,128)(2,1)S(1)}, f32[8,1024]{1,0:T(8,128)S(1)}) custom-call(bf16[1024,2048]{1,0:T(8,128)(2,1)} %bitcast.8.back_ref, bf16[256,1024]{1,0:T(8,128)(2,1)S(1)} %pad_maximum_fusion.mix_ref, bf16[128,2048]{1,0:T(8,128)(2,1)S(1)} %copy-done.1, bf16[3,128,2048]{2,1,0:T(8,128)(2,1)S(1)} %copy-done.2, ...), custom_call_target="tpu_custom_call" | custom-call | tf_op jit(solution)/shard_map/pallas_call | solution.py:249
  413.5 0.8 copy.34
  414.3 0.6 copy.35
  (27 shorter events, 1.1 us)
Async XLA Ops:
  7.2 3.5 copy-start
  7.2 6.9 %copy-start.1 = (bf16[128,2048]{1,0:T(8,128)(2,1)S(1)}, bf16[128,2048]{1,0:T(8,128)(2,1)}, u32[]{:S(2)}) copy-start(bf16[128,2048]{1,0:T(8,128)(2,1)} %hidden_ref.1) | copy-start | bytes 1572868
  7.2 6.9 %copy-start.5 = (f32[2048]{0:T(1024)S(1)}, f32[2048]{0:T(1024)}, u32[]{:S(2)}) copy-start(f32[2048]{0:T(1024)} %param.11) | copy-start | bytes 24580
  7.2 118.0 %all-gather.7.cloned.1.call-start = ((), (), s32[]{:S(2)}) async-start(), calls=%async_computation.2 | async-start | bytes 7208960 | tf_op jit(solution)/shard_map/all_gather | solution.py:336
  7.9 135.9 %all-gather.11.cloned.1.call-start = ((), (), s32[]{:S(2)}) async-start(), calls=%async_computation.4 | async-start | bytes 7208960 | tf_op jit(solution)/shard_map/all_gather | solution.py:344
  17.4 107.8 %all-to-all-start = ((bf16[64,16,2048]{2,1,0:T(8,128)(2,1)}), bf16[64,16,2048]{2,1,0:T(8,128)(2,1)}, u32[]{:S(2)}, u32[]{:S(2)}) async-start(bf16[64,16,2048]{2,1,0:T(8,128)(2,1)} %bitcast.36), calls=%async_computation | async-start | bytes 8388608 | tf_op jit(solution)/shard_map/all_to_all | solution.py:326
  30.7 179.4 %all-gather.9.cloned.1.call-start = ((), (), s32[]{:S(2)}) async-start(), calls=%async_computation.3 | async-start | bytes 7208960 | tf_op jit(solution)/shard_map/all_gather | solution.py:339
  230.8 11.1 %copy-start.4 = (bf16[128,2048]{1,0:T(8,128)(2,1)S(1)}, bf16[128,2048]{1,0:T(8,128)(2,1)}, u32[]{:S(2)}) copy-start(bf16[128,2048]{1,0:T(8,128)(2,1)} %param.18) | copy-start | bytes 1572868
  230.8 105.5 %copy-start.2 = (bf16[3,128,2048]{2,1,0:T(8,128)(2,1)S(1)}, bf16[3,128,2048]{2,1,0:T(8,128)(2,1)}, u32[]{:S(2)}) copy-start(bf16[3,128,2048]{2,1,0:T(8,128)(2,1)} %cached_ref.1) | copy-start | bytes 4718596
  230.8 105.5 %all-to-all-start.1 = ((bf16[64,16,2048]{2,1,0:T(8,128)(2,1)}), bf16[64,16,2048]{2,1,0:T(8,128)(2,1)}, u32[]{:S(2)}, u32[]{:S(2)}) async-start(bf16[64,16,2048]{2,1,0:T(8,128)(2,1)} %bitcast.37), calls=%async_computation.1 | async-start | bytes 8388608 | tf_op jit(solution)/shard_map/all_to_all | solution.py:326
  336.3 1.0 copy-start.3
Sparse Core Ops, SparseCore 0:
  9.8 67.6 all-gather.6
  79.3 64.4 all-gather.10
  145.7 64.4 all-gather.8

commit v2 on v1

--- a/solution.py
+++ b/solution.py
@@ -64,17 +64,37 @@
     return [jnp.sum(values, axis=0, keepdims=True), jnp.sum(values * values, axis=0, keepdims=True)]
 
 
-def tail_kernel(
+SLOTS = 16
+CHUNK = 512
+TILE = 256
+
+
+def kernel(
     total_tokens,
-    back_ref,
+    outgoing_ref,
     mix_ref,
     hidden_ref,
     cached_ref,
     prediction_ref,
     student_ref,
+    wg_ref,
+    wu_ref,
+    wd_ref,
     targets_ref,
     grad_ref,
+    wg,
+    wu,
+    wd,
+    arrived,
+    act,
+    out,
+    back,
     layer_out,
+    cached_own,
+    cached_c,
+    cached_x,
+    cached_y,
+    cached_z,
     stat_own,
     stat_c,
     stat_x,
@@ -86,6 +106,10 @@
     from_c,
     from_y,
     from_z,
+    sem_own,
+    sem_w,
+    sem_rows,
+    sem_back,
     sem_st,
     sem_s,
     sem_x,
@@ -96,19 +120,110 @@
     axes = wheel()
     tok, width = hidden_ref.shape
     window = prediction_ref.shape[1]
-    x = axes["x"][0]
-    c = axes["c"][0]
+    e, x, c = lax.axis_index("expert"), lax.axis_index("seq"), lax.axis_index("dp")
+    nx = axes["x"][1]
+    n = 2 * lax.axis_size("expert")
+    me = 2 * e + c
+    half = width // 2
+
+    def peer(d):
+        p = lax.rem(me + d, n)
+        return p, {"expert": p // 2, "seq": x, "dp": lax.rem(p, 2)}
 
     barrier = pltpu.get_barrier_semaphore()
-    greeted = 0
-    for name in "cxyz":
-        _, n, device = axes[name]
-        for d in range(1, n):
-            pl.semaphore_signal(barrier, inc=1, device_id=device(d), device_id_type=MESH)
-            greeted += 1
-    pl.semaphore_wait(barrier, greeted)
-
-    nx = axes["x"][1]
+
+    def greet(d, _):
+        pl.semaphore_signal(barrier, inc=1, device_id=peer(d)[1], device_id_type=MESH)
+        return _
+
+    lax.fori_loop(1, n, greet, 0)
+    for d in range(1, nx):
+        pl.semaphore_signal(barrier, inc=1, device_id=axes["x"][2](d), device_id_type=MESH)
+    pl.semaphore_wait(barrier, n - 1 + nx - 1)
+
+    right, left = axes["x"][2](1), axes["x"][2](nx - 1)
+    before, after = lax.rem(x + nx - 1, nx), lax.rem(x + 1, nx)
+
+    def weight_piece(number, shard, whole, cols):
+        rows = shard.shape[0]
+        cut = rows // 2
+
+        def at(origin, part):
+            return pl.ds(pl.multiple_of(origin * rows + part * cut, 16), cut)
+
+        def copy(i, source, origin, part, device):
+            return pltpu.make_async_remote_copy(
+                src_ref=source,
+                dst_ref=whole.at[at(origin, part), cols],
+                send_sem=sem_w.at[number, 0, i],
+                recv_sem=sem_w.at[number, 1, i],
+                device_id=device,
+                device_id_type=MESH,
+            )
+
+        def own(part):
+            return shard.at[pl.ds(part * cut, cut), cols]
+
+        def passed(origin, part):
+            return whole.at[at(origin, part), cols]
+
+        return [
+            copy(0, own(0), x, 0, right),
+            copy(1, own(1), x, 1, right),
+            copy(2, own(1), x, 1, left),
+            copy(3, own(0), x, 0, left),
+            copy(4, passed(before, 0), before, 0, right),
+            copy(5, passed(after, 1), after, 1, left),
+        ]
+
+    def begin(piece):
+        for i in (0, 2, 1, 3):
+            piece[i].start()
+
+    def pass_on(piece):
+        piece[0].wait_recv()
+        piece[4].start()
+        piece[2].wait_recv()
+        piece[5].start()
+
+    every = slice(0, wg.shape[1])
+    gate_piece = weight_piece(0, wg_ref, wg, every)
+    up_piece = weight_piece(1, wu_ref, wu, every)
+    down_pieces = [weight_piece(2 + i, wd_ref, wd, slice(i * half, (i + 1) * half)) for i in range(2)]
+    begin(gate_piece)
+
+    def block(p):
+        return pl.ds(pl.multiple_of(p * SLOTS, SLOTS), SLOTS)
+
+    def scatter(source, target, send, recv):
+        def go(d, _):
+            p, device = peer(d)
+            pltpu.make_async_remote_copy(
+                src_ref=source.at[block(p)],
+                dst_ref=target.at[block(me)],
+                send_sem=send,
+                recv_sem=recv,
+                device_id=device,
+                device_id_type=MESH,
+            ).start()
+            return _
+
+        lax.fori_loop(1, n, go, 0)
+        target[block(me), :] = source[block(me), :]
+
+    def wait_rows(ref, sem):
+        rows = ref.at[pl.ds(0, (n - 1) * SLOTS)]
+        pltpu.make_async_copy(rows, rows, sem).wait()
+
+    scatter(outgoing_ref, arrived, sem_rows.at[0], sem_rows.at[1])
+    mine = []
+    for i, (shard, whole) in enumerate(((wg_ref, wg), (wu_ref, wu), (wd_ref, wd))):
+        rows = shard.shape[0]
+        copy = pltpu.make_async_copy(
+            shard, whole.at[pl.ds(pl.multiple_of(x * rows, 16), rows)], sem_own.at[i]
+        )
+        copy.start()
+        mine.append(copy)
     students_out = start_all(
         axes["x"],
         lambda d: student_ref.at[lax.rem(x + d, nx)],
@@ -116,51 +231,119 @@
         sem_st.at[0],
         sem_st.at[1],
     )
+    students[0] = student_ref[x]
+
+    def add_over_devices(number, own, slots):
+        for i, name in enumerate("cxyz"):
+            copies = start_all(
+                axes[name],
+                lambda d: own.at[i],
+                lambda d: slots[i].at[d - 1],
+                sem_s.at[number, i, 0],
+                sem_s.at[number, i, 1],
+            )
+            wait_all(copies)
+            total = own[i]
+            for d in range(1, axes[name][1]):
+                total = total + slots[i][d - 1]
+            own[i + 1] = total
 
     stats = []
     for layer in range(3):
         stats += column_sums(cached_ref[layer].astype(F32))
-    cut = 512
-    for j in range(width // cut):
-        cols = slice(j * cut, (j + 1) * cut)
-        both = jnp.dot(mix_ref[...], back_ref[:, cols], preferred_element_type=F32)
-        layer_out[:, cols] = hidden_ref[:, cols].astype(F32) + (both[:tok] + both[tok:])
-    stats += column_sums(layer_out[...])
-    stat_own[0] = fold(stats)
-    for i, (name, slots) in enumerate((("c", stat_c), ("x", stat_x), ("y", stat_y), ("z", stat_z))):
-        copies = start_all(
-            axes[name],
-            lambda d, i=i: stat_own.at[i],
-            lambda d, slots=slots: slots.at[d - 1],
-            sem_s.at[i, 0],
-            sem_s.at[i, 1],
-        )
-        for copy in copies:
-            copy.wait_recv()
-        total = stat_own[i]
-        for d in range(1, axes[name][1]):
-            total = total + slots[d - 1]
-        stat_own[i + 1] = total
-        for copy in copies:
-            copy.wait_send()
-    total = stat_own[4]
-    for j in range(width // cut):
-        cols = slice(j * cut, (j + 1) * cut)
-        summed = jnp.zeros((tok, cut), F32)
-        for layer in range(4):
-            mean = total[8 * layer + j : 8 * layer + j + 1, :] / total_tokens
-            square = total[8 * layer + 4 + j : 8 * layer + 5 + j, :] / total_tokens
-            inverse = lax.rsqrt(square - mean * mean + 1e-5)
-            values = cached_ref[layer, :, cols].astype(F32) if layer < 3 else layer_out[:, cols]
-            summed = summed + (values - mean) * inverse
-        targets = (summed * 0.25).astype(BF16)
-        targets_ref[:, cols] = targets
-        if (j + 1) * cut <= window:
-            scale = 1.0 / math.sqrt(total_tokens)
-            residuals[0, :, cols] = (
-                (prediction_ref[:, cols].astype(F32) - targets.astype(F32)) * scale
+    cached_own[0] = fold(stats)
+
+    pass_on(gate_piece)
+    gate_piece[1].wait_recv()
+    gate_piece[3].wait_recv()
+    begin(up_piece)
+    add_over_devices(0, cached_own, (cached_c, cached_x, cached_y, cached_z))
+    pass_on(up_piece)
+    gate_piece[4].wait_recv()
+    gate_piece[5].wait_recv()
+    up_piece[1].wait_recv()
+    up_piece[3].wait_recv()
+    begin(down_pieces[0])
+    up_piece[4].wait_recv()
+    up_piece[5].wait_recv()
+    for copy in mine:
+        copy.wait()
+    wait_rows(arrived, sem_rows.at[1])
+
+    def activate(i, _):
+        at = pl.ds(pl.multiple_of(i * TILE, TILE), TILE)
+        gate = jnp.dot(arrived[at, :], wg[...], preferred_element_type=F32)
+        up = jnp.dot(arrived[at, :], wu[...], preferred_element_type=F32)
+        act[at, :] = (gate * jax.nn.sigmoid(gate) * up).astype(BF16)
+        return _
+
+    tiles = arrived.shape[0] // TILE
+    lax.fori_loop(0, tiles // 2, activate, 0)
+    pass_on(down_pieces[0])
+    lax.fori_loop(tiles // 2, tiles, activate, 0)
+    down_pieces[0][1].wait_recv()
+    down_pieces[0][3].wait_recv()
+    begin(down_pieces[1])
+    down_pieces[0][4].wait_recv()
+    down_pieces[0][5].wait_recv()
+
+    chunks = width // CHUNK
+    for j in range(chunks):
+        if j == chunks // 2:
+            for i in (1, 3, 4, 5):
+                down_pieces[1][i].wait_recv()
+
+        def project(i, _):
+            at = pl.ds(pl.multiple_of(i * TILE, TILE), TILE)
+            out[j, at, :] = jnp.dot(
+                act[at, :], wd[:, j * CHUNK : (j + 1) * CHUNK], preferred_element_type=F32
             ).astype(BF16)
-
+            return _
+
+        lax.fori_loop(0, tiles, project, 0)
+        scatter(out.at[j], back.at[j], sem_back.at[0, j], sem_back.at[1, j])
+        if j == chunks // 2 - 1:
+            pass_on(down_pieces[1])
+
+    scale = 1.0 / math.sqrt(total_tokens)
+    tail_cut = 4
+
+    def finish(h):
+        for j in range(h * chunks // 2, (h + 1) * chunks // 2):
+            wait_rows(back.at[j], sem_back.at[1, j])
+            cols = slice(j * CHUNK, (j + 1) * CHUNK)
+            both = jnp.dot(mix_ref[...], back[j], preferred_element_type=F32)
+            layer_out[:, cols] = hidden_ref[:, cols].astype(F32) + (both[:tok] + both[tok:])
+        stat_own[h, 0] = fold(column_sums(layer_out[:, h * half : (h + 1) * half]))
+        slots = [s.at[h] for s in (stat_c, stat_x, stat_y, stat_z)]
+        add_over_devices(1 + h, stat_own.at[h], slots)
+        last = stat_own[h, 4]
+        earlier = cached_own[4]
+        w = half // tail_cut
+        for j in range(h * chunks // 2, (h + 1) * chunks // 2):
+            cols = slice(j * CHUNK, (j + 1) * CHUNK)
+            summed = jnp.zeros((tok, CHUNK), F32)
+            for layer in range(4):
+                if layer < 3:
+                    sums = earlier[8 * layer + j : 8 * layer + j + 1, :]
+                    squares = earlier[8 * layer + 4 + j : 8 * layer + 5 + j, :]
+                    values = cached_ref[layer, :, cols].astype(F32)
+                else:
+                    k = (j - h * chunks // 2) * (CHUNK // w)
+                    sums = jnp.concatenate([last[k : k + 1], last[k + 1 : k + 2]], axis=1)
+                    squares = jnp.concatenate([last[4 + k : 5 + k], last[5 + k : 6 + k]], axis=1)
+                    values = layer_out[:, cols]
+                mean = sums / total_tokens
+                variance = squares / total_tokens - mean * mean
+                summed = summed + (values - mean) * lax.rsqrt(variance + 1e-5)
+            targets = (summed * 0.25).astype(BF16)
+            targets_ref[:, cols] = targets
+            if (j + 1) * CHUNK <= window:
+                residuals[0, :, cols] = (
+                    (prediction_ref[:, cols].astype(F32) - targets.astype(F32)) * scale
+                ).astype(BF16)
+
+    finish(0)
     copies = start_all(
         axes["x"],
         lambda d: residuals.at[0],
@@ -168,11 +351,9 @@
         sem_x.at[0],
         sem_x.at[1],
     )
-    for copy in students_out:
-        copy.wait()
-    students[0] = student_ref[x]
+    wait_all(students_out)
     rows = partial.shape[0]
-    half = rows // 2
+    halved = rows // 2
     for d in range(nx):
         if d:
             copies[d - 1].wait_recv()
@@ -186,8 +367,8 @@
         lax.fori_loop(0, rows // 128, add, 0)
     for copy in copies:
         copy.wait_send()
-    other = pl.ds(pl.multiple_of((1 - c) * half, half), half)
-    mine = pl.ds(pl.multiple_of(c * half, half), half)
+    other = pl.ds(pl.multiple_of((1 - c) * halved, halved), halved)
+    kept = pl.ds(pl.multiple_of(c * halved, halved), halved)
     wait_all(
         start_all(
             axes["c"],
@@ -197,9 +378,9 @@
             sem_c.at[1],
         )
     )
-    from_c[...] = from_c[...] + partial[mine, :]
+    from_c[...] = from_c[...] + partial[kept, :]
     y, ny, _ = axes["y"]
-    part = half // ny
+    part = halved // ny
 
     def y_rows(d):
         return pl.ds(pl.multiple_of(lax.rem(y + d, ny) * part, part), part)
@@ -237,50 +418,75 @@
         total = total + from_z[d]
     grad_ref[...] = total
 
-
-def tail(total_tokens, back, mix, hidden_in, cached, prediction, student):
+    finish(1)
+    for piece in (gate_piece, up_piece, *down_pieces):
+        for copy in piece:
+            copy.wait_send()
+    wait_rows(outgoing_ref, sem_rows.at[0])
+    for j in range(chunks):
+        wait_rows(out.at[j], sem_back.at[0, j])
+
+
+def run(total_tokens, outgoing, mix, hidden_in, cached, prediction, student, wg, wu, wd):
     tok, width = hidden_in.shape
     window = prediction.shape[1]
     nx, ny, nz = lax.axis_size("seq"), NY, lax.axis_size("expert") // NY
     rows = width // nx
+    hidden_units = wg.shape[1]
+    arrived = outgoing.shape[0]
+    chunks = width // CHUNK
     vmem = pl.BlockSpec(memory_space=pltpu.VMEM)
+    hbm = pl.BlockSpec(memory_space=pl.ANY)
     dma = pltpu.SemaphoreType.DMA
-    stat = (32, width // 4)
+    early, late = (24, width // 4), (8, width // 8)
     return pl.pallas_call(
-        functools.partial(tail_kernel, total_tokens),
+        functools.partial(kernel, total_tokens),
         out_shape=(
             jax.ShapeDtypeStruct((tok, width), BF16),
             jax.ShapeDtypeStruct((rows // (2 * ny * nz), window), F32),
         ),
-        in_specs=[vmem] * 6,
+        in_specs=[vmem] * 6 + [hbm] * 3,
         out_specs=(vmem, vmem),
         scratch_shapes=[
+            pltpu.VMEM((width, hidden_units), BF16),
+            pltpu.VMEM((width, hidden_units), BF16),
+            pltpu.VMEM((hidden_units, width), BF16),
+            pltpu.VMEM((arrived, width), BF16),
+            pltpu.VMEM((arrived, hidden_units), BF16),
+            pltpu.VMEM((chunks, arrived, CHUNK), BF16),
+            pltpu.VMEM((chunks, arrived, CHUNK), BF16),
             pltpu.VMEM((tok, width), F32),
-            pltpu.VMEM((5, *stat), F32),
-            pltpu.VMEM((1, *stat), F32),
-            pltpu.VMEM((nx - 1, *stat), F32),
-            pltpu.VMEM((ny - 1, *stat), F32),
-            pltpu.VMEM((nz - 1, *stat), F32),
+            pltpu.VMEM((5, *early), F32),
+            pltpu.VMEM((1, *early), F32),
+            pltpu.VMEM((nx - 1, *early), F32),
+            pltpu.VMEM((ny - 1, *early), F32),
+            pltpu.VMEM((nz - 1, *early), F32),
+            pltpu.VMEM((2, 5, *late), F32),
+            pltpu.VMEM((2, 1, *late), F32),
+            pltpu.VMEM((2, nx - 1, *late), F32),
+            pltpu.VMEM((2, ny - 1, *late), F32),
+            pltpu.VMEM((2, nz - 1, *late), F32),
             pltpu.VMEM((nx, rows, tok), BF16),
             pltpu.VMEM((nx, tok, window), BF16),
             pltpu.VMEM((rows, window), F32),
             pltpu.VMEM((rows // 2, window), F32),
             pltpu.VMEM((ny, rows // (2 * ny), window), F32),
             pltpu.VMEM((nz, rows // (2 * ny * nz), window), F32),
+            dma((3,)),
+            dma((4, 2, 6)),
+            dma((2,)),
+            dma((2, chunks)),
             dma((2, nx - 1)),
-            dma((4, 2, 7)),
+            dma((3, 4, 2, 7)),
             dma((2, nx - 1)),
             dma((2, 1)),
             dma((2, ny - 1)),
             dma((2, nz - 1)),
         ],
         compiler_params=pltpu.CompilerParams(
-            collective_id=1, has_side_effects=True, vmem_limit_bytes=40 * 2**20
+            collective_id=1, has_side_effects=True, vmem_limit_bytes=60 * 2**20
         ),
-    )(back, mix, hidden_in, cached, prediction, student)
-
-
-SLOTS = 16
+    )(outgoing, mix, hidden_in, cached, prediction, student, wg, wu, wd)
 
 
 def body(
@@ -322,35 +528,23 @@
         pick, normed, (((0,), (0,)), ((), ())), preferred_element_type=F32
     ).astype(BF16)
 
-    def exchange(rows):
-        return lax.all_to_all(
-            rows.reshape(n_experts, SLOTS, width),
-            ("expert", "dp"),
-            split_axis=0,
-            concat_axis=0,
-            tiled=True,
-        ).reshape(n_experts * SLOTS, width)
-
-    rows = exchange(outgoing)
-    gate_acc = jnp.dot(
-        rows, lax.all_gather(w_gate[0], "seq", axis=0, tiled=True), preferred_element_type=F32
-    )
-    up_acc = jnp.dot(
-        rows, lax.all_gather(w_up[0], "seq", axis=0, tiled=True), preferred_element_type=F32
-    )
-    activation = (jax.nn.silu(gate_acc) * up_acc).astype(BF16)
-    expert_out = jnp.dot(
-        activation,
-        lax.all_gather(w_down[0], "seq", axis=0, tiled=True),
-        preferred_element_type=F32,
-    ).astype(BF16)
-    back = exchange(expert_out)
     student = (
         student_hidden.T.reshape(nz, NY, nx, 2, width // (2 * nx * NY * nz), tok)
         .transpose(2, 3, 1, 0, 4, 5)
         .reshape(nx, width // nx, tok)
     )
-    return tail(total_tokens, back, mix, hidden_in, cached_layers, prediction, student)
+    return run(
+        total_tokens,
+        outgoing,
+        mix,
+        hidden_in,
+        cached_layers,
+        prediction,
+        student,
+        w_gate[0],
+        w_up[0],
+        w_down[0],
+    )
 
 
 def solution(mesh):

time: 422 us -> 337 us (0.80)
  waiting for transfers between devices: 260 us -> 0 us
  Pallas kernels: 76.3 us -> 321 us
  matrix products: 37.3 us -> 4.92 us
  starting transfers between devices: 24.5 us -> 0 us
  between operations: 13.9 us -> 0.77 us
    pallas_call x1, Pallas kernels: 76.3 us -> 321 us  [run(): pl.pallas_call(functools.partial(kernel, total_tokens), out_shape=(jax.Sh...]
    all_to_all x2 -> x0, waiting for transfers between devices: 185 us -> none  [exchange(): lax.all_to_all(rows.reshape(n_experts, SLOTS, width), ('expert', 'dp'), s...]
    all_gather x3 -> x0, waiting for transfers between devices: 73.3 us -> none  [the longest x1 66.3 us: body(): lax.all_gather(w_up[0], 'seq', axis=0, tiled=True)]
    dot_general x2 -> x0, matrix products: 32.4 us -> none  [the longest x1 20.6 us: body(): jnp.dot(activation, lax.all_gather(w_down[0], 'seq', axis=0, tiled=True),...]
    all_to_all x2 -> x0, starting transfers between devices: 24.4 us -> none  [exchange(): lax.all_to_all(rows.reshape(n_experts, SLOTS, width), ('expert', 'dp'), s...]
  transfers between devices with their start and end apart: 5 -> 0, of which waited for: 4 -> 0; matrix products, arithmetic and copies ran while one was open for 6% -> 0% of each run, Pallas kernels for 0% -> 0%
where the time goes in v2:
time: 337 us; the launch traced here: 335 us
  Pallas kernels  321 us (95%)
  local copies, waits for them, and re-layouts  5.3 us (2%)
  matrix products  4.92 us (1%)
    pallas_call x1, Pallas kernels, run(): pl.pallas_call(functools.partial(kernel, total_tokens), out_shape=(jax.Sh...  321 us

profile of v2, /device:TPU:1, one launch (start us, length us, event | category | flops | bytes accessed | tf_op | source)
XLA Modules:
  0.0 335.0 jit_solution(14853834162593074071)
XLA Ops:
  0.6 0.0 copy-start
  0.6 1.3 fusion.4
  1.9 0.7 fusion.7
  2.7 0.2 fusion.11
  2.9 0.1 eq.40
  3.0 0.0 copy-done
  3.0 1.4 fusion.18
  4.5 0.2 copy.24
  4.7 0.2 copy.25
  5.0 0.2 copy.23
  5.2 0.0 copy-start.2
  5.2 0.2 select_convert_fusion
  5.4 0.1 subtract_convert_fusion
  5.4 0.0 copy-start.1
  5.5 0.0 copy-start.3
  5.5 0.8 pad_maximum_fusion.mix_ref
  6.3 0.0 copy-done.2
  6.3 0.3 copy.26
  6.6 0.9 copy.27
  7.5 0.0 copy-done.1
  7.5 3.3 convolution_convert_fusion.outgoing_ref
  10.8 320.9 %shard_map.113 = (bf16[128,2048]{1,0:T(8,128)(2,1)}, f32[8,1024]{1,0:T(8,128)}) custom-call(bf16[1024,2048]{1,0:T(8,128)(2,1)} %convolution_convert_fusion.outgoing_ref, bf16[256,1024]{1,0:T(8,128)(2,1)} %pad_maximum_fusion.mix_ref, bf16[128,2048]{1,0:T(8,128)(2,1)} %hidden_ref.1, bf16[3,128,2048]{2,1,0:T(8,128)(2,1)} %cached_ref.1, ...), custom_call_target="tpu_custom_call" | custom-call | tf_op jit(solution)/shard_map/pallas_call | solution.py:442
  331.7 1.9 copy.34
  333.6 1.4 copy.35
  (8 shorter events, 0.1 us)
Async XLA Ops:
  0.6 2.3 copy-start
  5.2 1.1 copy-start.2
  5.4 2.1 copy-start.1
  5.5 2.1 copy-start.3

commit v3 on v2

--- a/solution.py
+++ b/solution.py
@@ -15,15 +15,19 @@
 
 def wheel():
     e, x, c = lax.axis_index("expert"), lax.axis_index("seq"), lax.axis_index("dp")
-    nz = lax.axis_size("expert") // NY
+    nx, nz = lax.axis_size("seq"), lax.axis_size("expert") // NY
     z, y = e // NY, lax.rem(e, NY)
 
     def to(z_, y_, x_, c_):
         return {"expert": z_ * NY + y_, "seq": x_, "dp": c_}
 
+    def beside(q):
+        return to(z, y, q // 2, lax.rem(q, 2))
+
     return {
         "c": (c, 2, lambda d: to(z, y, x, lax.rem(c + d, 2))),
-        "x": (x, lax.axis_size("seq"), lambda d: to(z, y, lax.rem(x + d, lax.axis_size("seq")), c)),
+        "w": (2 * x + c, 2 * nx, lambda d: beside(lax.rem(2 * x + c + d, 2 * nx))),
+        "x": (x, nx, lambda d: to(z, y, lax.rem(x + d, nx), c)),
         "y": (y, NY, lambda d: to(z, lax.rem(y + d, NY), x, c)),
         "z": (z, nz, lambda d: to(lax.rem(z + d, nz), y, x, c)),
     }
@@ -69,10 +73,58 @@
 TILE = 256
 
 
+def normalise(hidden_ref, gain_ref, router_ref):
+    hidden = hidden_ref[...].astype(F32)
+    mean = jnp.mean(hidden * hidden, axis=-1, keepdims=True)
+    normed = (hidden * lax.rsqrt(mean + 1e-6) * gain_ref[...]).astype(BF16)
+    logits = lax.dot_general(
+        normed, router_ref[...], (((1,), (1,)), ((), ())), preferred_element_type=F32
+    )
+    return normed, logits
+
+
+def choose(routes_ref, logits, pick_ref, mix_ref):
+    top, tok = routes_ref.shape
+    experts = logits.shape[1]
+
+    def index(shape, dim):
+        return lax.broadcasted_iota(jnp.int32, shape, dim)
+
+    def ones(flags):
+        return jnp.where(flags, 1.0, 0.0)
+
+    names = index((experts, tok), 0)
+    chosen = jnp.zeros((experts, tok), F32)
+    for k in range(top):
+        chosen = chosen + ones(names == routes_ref[k : k + 1, :])
+    square = (tok, tok)
+    earlier = ones(index(square, 0) < index(square, 1)).astype(BF16)
+    place = jnp.dot(chosen.astype(BF16), earlier, preferred_element_type=F32)
+    code = jnp.where(chosen > 0.5, place, -1.0).astype(BF16)
+    same = ones(index(square, 0) == index(square, 1)).astype(BF16)
+    code_of = lax.dot_general(same, code, (((1,), (1,)), ((), ())), preferred_element_type=F32)
+    tall, wide = (experts * SLOTS, experts), (experts, experts * SLOTS)
+    spread_rows = ones(index(tall, 0) // SLOTS == index(tall, 1)).astype(BF16)
+    spread = ones(index(wide, 1) // SLOTS == index(wide, 0)).astype(BF16)
+    rows = jnp.dot(spread_rows, code, preferred_element_type=F32)
+    slots = lax.rem(index(rows.shape, 0), SLOTS).astype(F32)
+    pick_ref[...] = ones(rows == slots).astype(BF16)
+    affinity = jnp.where(code_of > -0.5, jax.nn.sigmoid(logits), 0.0)
+    share = affinity / jnp.sum(affinity, axis=-1, keepdims=True)
+    high = share.astype(BF16)
+    low = (share - high.astype(F32)).astype(BF16)
+    columns = jnp.dot(code_of.astype(BF16), spread, preferred_element_type=F32)
+    match = columns == lax.rem(index(columns.shape, 1), SLOTS).astype(F32)
+    for i, part in enumerate((high, low)):
+        shares = jnp.dot(part, spread, preferred_element_type=F32)
+        mix_ref[i * tok : (i + 1) * tok, :] = jnp.where(match, shares, 0.0).astype(BF16)
+
+
 def kernel(
     total_tokens,
-    outgoing_ref,
-    mix_ref,
+    gain_ref,
+    router_ref,
+    routes_ref,
     hidden_ref,
     cached_ref,
     prediction_ref,
@@ -85,29 +137,34 @@
     wg,
     wu,
     wd,
+    pick_ref,
+    mix_ref,
+    blocks,
+    picks,
     arrived,
+    gated,
+    raised,
     act,
     out,
     back,
     layer_out,
     cached_own,
-    cached_c,
-    cached_x,
+    cached_w,
     cached_y,
     cached_z,
     stat_own,
-    stat_c,
-    stat_x,
+    stat_w,
     stat_y,
     stat_z,
     students,
     residuals,
-    partial,
     from_c,
     from_y,
     from_z,
     sem_own,
     sem_w,
+    sem_ring,
+    sem_pick,
     sem_rows,
     sem_back,
     sem_st,
@@ -125,6 +182,8 @@
     n = 2 * lax.axis_size("expert")
     me = 2 * e + c
     half = width // 2
+    z, nz, z_device = axes["z"]
+    y, ny, _ = axes["y"]
 
     def peer(d):
         p = lax.rem(me + d, n)
@@ -137,9 +196,9 @@
         return _
 
     lax.fori_loop(1, n, greet, 0)
-    for d in range(1, nx):
-        pl.semaphore_signal(barrier, inc=1, device_id=axes["x"][2](d), device_id_type=MESH)
-    pl.semaphore_wait(barrier, n - 1 + nx - 1)
+    for d in range(1, 2 * nx):
+        pl.semaphore_signal(barrier, inc=1, device_id=axes["w"][2](d), device_id_type=MESH)
+    pl.semaphore_wait(barrier, n - 1 + 2 * nx - 1)
 
     right, left = axes["x"][2](1), axes["x"][2](nx - 1)
     before, after = lax.rem(x + nx - 1, nx), lax.rem(x + 1, nx)
@@ -189,18 +248,23 @@
     every = slice(0, wg.shape[1])
     gate_piece = weight_piece(0, wg_ref, wg, every)
     up_piece = weight_piece(1, wu_ref, wu, every)
-    down_pieces = [weight_piece(2 + i, wd_ref, wd, slice(i * half, (i + 1) * half)) for i in range(2)]
+    chunks = width // CHUNK
+    down_pieces = [
+        weight_piece(2 + i, wd_ref, wd, slice(i * CHUNK, (i + 1) * CHUNK)) for i in range(chunks)
+    ]
     begin(gate_piece)
+    blocks[z], logits = normalise(hidden_ref, gain_ref, router_ref)
+    choose(routes_ref, logits, pick_ref, mix_ref)
 
     def block(p):
         return pl.ds(pl.multiple_of(p * SLOTS, SLOTS), SLOTS)
 
-    def scatter(source, target, send, recv):
+    def scatter(source, target, cols, send, recv):
         def go(d, _):
             p, device = peer(d)
             pltpu.make_async_remote_copy(
-                src_ref=source.at[block(p)],
-                dst_ref=target.at[block(me)],
+                src_ref=source.at[block(p), cols],
+                dst_ref=target.at[block(me), cols],
                 send_sem=send,
                 recv_sem=recv,
                 device_id=device,
@@ -209,13 +273,77 @@
             return _
 
         lax.fori_loop(1, n, go, 0)
-        target[block(me), :] = source[block(me), :]
-
-    def wait_rows(ref, sem):
-        rows = ref.at[pl.ds(0, (n - 1) * SLOTS)]
+        target[block(me), cols] = source[block(me), cols]
+
+    def wait_rows(ref, count, cols, sem):
+        rows = ref.at[pl.ds(0, count * SLOTS), cols]
         pltpu.make_async_copy(rows, rows, sem).wait()
 
-    scatter(outgoing_ref, arrived, sem_rows.at[0], sem_rows.at[1])
+    group = 2 * ny * SLOTS
+    half_block = tok // 2
+    last = nz - 2
+
+    def ring(way, m):
+        s, part = m // 2, (m + way) % 2
+        b = lax.rem(z + (nz - s if way == 0 else s), nz)
+        rows = blocks.at[b, pl.ds(part * half_block, half_block)]
+        return pltpu.make_async_remote_copy(
+            src_ref=rows,
+            dst_ref=rows,
+            send_sem=sem_ring.at[0, way, m],
+            recv_sem=sem_ring.at[1, way, m],
+            device_id=z_device(1 if way == 0 else nz - 1),
+            device_id_type=MESH,
+        )
+
+    rings = [[ring(way, m) for m in range(last + 1)] for way in range(2)]
+
+    def group_rows(b):
+        return pl.ds(pl.multiple_of(b * group, group), group)
+
+    def start_ring(m):
+        for way in range(2):
+            rings[way][m].start()
+
+    def next_ring(m):
+        for way in range(2):
+            rings[way][m].wait_recv()
+            if m + 2 <= last:
+                rings[way][m + 2].start()
+
+    def select(b):
+        for j in range(chunks):
+            cols = slice(j * CHUNK, (j + 1) * CHUNK)
+            out[group_rows(b), cols] = jnp.dot(
+                picks[b], blocks[b, :, cols], preferred_element_type=F32
+            ).astype(BF16)
+        p = (b * ny + y) * 2 + c
+
+        def go(d, _):
+            q = lax.rem(2 * y + c + d, 2 * ny)
+            pltpu.make_async_remote_copy(
+                src_ref=out.at[block(b * 2 * ny + q)],
+                dst_ref=arrived.at[block(p)],
+                send_sem=sem_rows.at[0],
+                recv_sem=sem_rows.at[1],
+                device_id={"expert": z * ny + q // 2, "seq": x, "dp": lax.rem(q, 2)},
+                device_id_type=MESH,
+            ).start()
+            return _
+
+        lax.fori_loop(1, 2 * ny, go, 0)
+        arrived[block(p), :] = out[block(b * 2 * ny + 2 * y + c), :]
+
+    picks_out = start_all(
+        axes["z"],
+        lambda d: pick_ref.at[group_rows(lax.rem(z + d, nz))],
+        lambda d: picks.at[z],
+        sem_pick.at[0],
+        sem_pick.at[1],
+    )
+    start_ring(0)
+    start_ring(1)
+    picks[z] = pick_ref[group_rows(z), :]
     mine = []
     for i, (shard, whole) in enumerate(((wg_ref, wg), (wu_ref, wu), (wd_ref, wd))):
         rows = shard.shape[0]
@@ -234,7 +362,7 @@
     students[0] = student_ref[x]
 
     def add_over_devices(number, own, slots):
-        for i, name in enumerate("cxyz"):
+        for i, name in enumerate("wyz"):
             copies = start_all(
                 axes[name],
                 lambda d: own.at[i],
@@ -253,72 +381,117 @@
         stats += column_sums(cached_ref[layer].astype(F32))
     cached_own[0] = fold(stats)
 
+    for copy in picks_out:
+        copy.wait_recv()
+    select(z)
+    for m in range(2):
+        next_ring(m)
+    select(lax.rem(z + nz - 1, nz))
+    select(lax.rem(z + 1, nz))
+    for m in range(2, 4):
+        next_ring(m)
+    select(lax.rem(z + nz - 2, nz))
+    select(lax.rem(z + 2, nz))
     pass_on(gate_piece)
+    for m in range(4, 6):
+        next_ring(m)
+    select(lax.rem(z + nz - 3, nz))
+    select(lax.rem(z + 3, nz))
     gate_piece[1].wait_recv()
     gate_piece[3].wait_recv()
     begin(up_piece)
-    add_over_devices(0, cached_own, (cached_c, cached_x, cached_y, cached_z))
-    pass_on(up_piece)
+    next_ring(6)
+    select(lax.rem(z + nz // 2, nz))
+    add_over_devices(0, cached_own, (cached_w, cached_y, cached_z))
+    for copy in mine:
+        copy.wait()
     gate_piece[4].wait_recv()
     gate_piece[5].wait_recv()
+    everything = slice(0, width)
+    wait_rows(arrived, n - nz, everything, sem_rows.at[1])
+
+    def gate_tile(i, _):
+        at = pl.ds(pl.multiple_of(i * TILE, TILE), TILE)
+        gate = jnp.dot(arrived[at, :], wg[...], preferred_element_type=F32)
+        gated[at, :] = gate * jax.nn.sigmoid(gate)
+        return _
+
+    shard = wu_ref.shape[0]
+
+    def up_part(at, origin):
+        rows = pl.ds(pl.multiple_of(origin * shard, shard), shard)
+        return jnp.dot(arrived[at, rows], wu[rows, :], preferred_element_type=F32)
+
+    def up_tile(i, _):
+        at = pl.ds(pl.multiple_of(i * TILE, TILE), TILE)
+        raised[at, :] = up_part(at, x) + up_part(at, before) + up_part(at, after)
+        return _
+
+    def act_tile(i, _):
+        at = pl.ds(pl.multiple_of(i * TILE, TILE), TILE)
+        up = raised[at, :] + up_part(at, lax.rem(x + 2, nx))
+        act[at, :] = (gated[at, :] * up).astype(BF16)
+        return _
+
+    tiles = arrived.shape[0] // TILE
+    lax.fori_loop(0, tiles // 2, gate_tile, 0)
+    pass_on(up_piece)
+    lax.fori_loop(tiles // 2, tiles, gate_tile, 0)
     up_piece[1].wait_recv()
     up_piece[3].wait_recv()
     begin(down_pieces[0])
+    lax.fori_loop(0, tiles, up_tile, 0)
     up_piece[4].wait_recv()
     up_piece[5].wait_recv()
-    for copy in mine:
-        copy.wait()
-    wait_rows(arrived, sem_rows.at[1])
-
-    def activate(i, _):
-        at = pl.ds(pl.multiple_of(i * TILE, TILE), TILE)
-        gate = jnp.dot(arrived[at, :], wg[...], preferred_element_type=F32)
-        up = jnp.dot(arrived[at, :], wu[...], preferred_element_type=F32)
-        act[at, :] = (gate * jax.nn.sigmoid(gate) * up).astype(BF16)
-        return _
-
-    tiles = arrived.shape[0] // TILE
-    lax.fori_loop(0, tiles // 2, activate, 0)
+    begin(down_pieces[1])
+    lax.fori_loop(0, tiles, act_tile, 0)
+    wait_rows(out, n - nz, everything, sem_rows.at[0])
     pass_on(down_pieces[0])
-    lax.fori_loop(tiles // 2, tiles, activate, 0)
-    down_pieces[0][1].wait_recv()
-    down_pieces[0][3].wait_recv()
-    begin(down_pieces[1])
-    down_pieces[0][4].wait_recv()
-    down_pieces[0][5].wait_recv()
-
-    chunks = width // CHUNK
+
+    def send_back(j):
+        cols = slice(j * CHUNK, (j + 1) * CHUNK)
+        scatter(out, back, cols, sem_back.at[0, j], sem_back.at[1, j])
+
     for j in range(chunks):
-        if j == chunks // 2:
-            for i in (1, 3, 4, 5):
-                down_pieces[1][i].wait_recv()
+        if j + 2 < chunks:
+            begin(down_pieces[j + 2])
+        for i in (1, 3, 4, 5):
+            down_pieces[j][i].wait_recv()
+        cols = slice(j * CHUNK, (j + 1) * CHUNK)
 
         def project(i, _):
             at = pl.ds(pl.multiple_of(i * TILE, TILE), TILE)
-            out[j, at, :] = jnp.dot(
-                act[at, :], wd[:, j * CHUNK : (j + 1) * CHUNK], preferred_element_type=F32
-            ).astype(BF16)
+            out[at, cols] = jnp.dot(act[at, :], wd[:, cols], preferred_element_type=F32).astype(BF16)
             return _
 
         lax.fori_loop(0, tiles, project, 0)
-        scatter(out.at[j], back.at[j], sem_back.at[0, j], sem_back.at[1, j])
-        if j == chunks // 2 - 1:
-            pass_on(down_pieces[1])
-
+        if j < chunks // 2:
+            send_back(j)
+        if j + 1 < chunks:
+            pass_on(down_pieces[j + 1])
+
+    for j in range(chunks // 2):
+        wait_rows(out, n - 1, slice(j * CHUNK, (j + 1) * CHUNK), sem_back.at[0, j])
+    for j in range(chunks // 2, chunks):
+        send_back(j)
     scale = 1.0 / math.sqrt(total_tokens)
     tail_cut = 4
 
-    def finish(h):
+    def combine(h):
         for j in range(h * chunks // 2, (h + 1) * chunks // 2):
-            wait_rows(back.at[j], sem_back.at[1, j])
             cols = slice(j * CHUNK, (j + 1) * CHUNK)
-            both = jnp.dot(mix_ref[...], back[j], preferred_element_type=F32)
+            wait_rows(back, n - 1, cols, sem_back.at[1, j])
+            both = jnp.dot(mix_ref[...], back[:, cols], preferred_element_type=F32)
             layer_out[:, cols] = hidden_ref[:, cols].astype(F32) + (both[:tok] + both[tok:])
         stat_own[h, 0] = fold(column_sums(layer_out[:, h * half : (h + 1) * half]))
-        slots = [s.at[h] for s in (stat_c, stat_x, stat_y, stat_z)]
+
+    def add_statistics(h):
+        slots = [s.at[h] for s in (stat_w, stat_y, stat_z)]
         add_over_devices(1 + h, stat_own.at[h], slots)
-        last = stat_own[h, 4]
-        earlier = cached_own[4]
+
+    def write_targets(h):
+        last = stat_own[h, 3]
+        earlier = cached_own[3]
         w = half // tail_cut
         for j in range(h * chunks // 2, (h + 1) * chunks // 2):
             cols = slice(j * CHUNK, (j + 1) * CHUNK)
@@ -343,7 +516,9 @@
                     (prediction_ref[:, cols].astype(F32) - targets.astype(F32)) * scale
                 ).astype(BF16)
 
-    finish(0)
+    combine(0)
+    add_statistics(0)
+    write_targets(0)
     copies = start_all(
         axes["x"],
         lambda d: residuals.at[0],
@@ -352,7 +527,8 @@
         sem_x.at[1],
     )
     wait_all(students_out)
-    rows = partial.shape[0]
+    rows = students.shape[1]
+    partial = raised.at[pl.ds(0, rows), pl.ds(0, window)]
     halved = rows // 2
     for d in range(nx):
         if d:
@@ -379,61 +555,60 @@
         )
     )
     from_c[...] = from_c[...] + partial[kept, :]
-    y, ny, _ = axes["y"]
     part = halved // ny
 
     def y_rows(d):
         return pl.ds(pl.multiple_of(lax.rem(y + d, ny) * part, part), part)
 
-    wait_all(
-        start_all(
-            axes["y"],
-            lambda d: from_c.at[y_rows(d)],
-            lambda d: from_y.at[d],
-            sem_y.at[0],
-            sem_y.at[1],
-        )
-    )
+    copies = start_all(
+        axes["y"],
+        lambda d: from_c.at[y_rows(d)],
+        lambda d: from_y.at[d],
+        sem_y.at[0],
+        sem_y.at[1],
+    )
+    combine(1)
+    add_statistics(1)
+    wait_all(copies)
     total = from_c[y_rows(0), :]
     for d in range(1, ny):
         total = total + from_y[d]
     from_y[0] = total
-    z, nz, _ = axes["z"]
     least = part // nz
 
     def z_rows(d):
         return pl.ds(pl.multiple_of(lax.rem(z + d, nz) * least, least), least)
 
-    wait_all(
-        start_all(
-            axes["z"],
-            lambda d: from_y.at[0, z_rows(d)],
-            lambda d: from_z.at[d],
-            sem_z.at[0],
-            sem_z.at[1],
-        )
-    )
+    copies = start_all(
+        axes["z"],
+        lambda d: from_y.at[0, z_rows(d)],
+        lambda d: from_z.at[d],
+        sem_z.at[0],
+        sem_z.at[1],
+    )
+    write_targets(1)
+    wait_all(copies)
     total = from_y[0, z_rows(0), :]
     for d in range(1, nz):
         total = total + from_z[d]
     grad_ref[...] = total
 
-    finish(1)
     for piece in (gate_piece, up_piece, *down_pieces):
         for copy in piece:
             copy.wait_send()
-    wait_rows(outgoing_ref, sem_rows.at[0])
-    for j in range(chunks):
-        wait_rows(out.at[j], sem_back.at[0, j])
-
-
-def run(total_tokens, outgoing, mix, hidden_in, cached, prediction, student, wg, wu, wd):
+    for copy in (*picks_out, *rings[0], *rings[1]):
+        copy.wait_send()
+    for j in range(chunks // 2, chunks):
+        wait_rows(out, n - 1, slice(j * CHUNK, (j + 1) * CHUNK), sem_back.at[0, j])
+
+
+def run(total_tokens, gain, router, routes, hidden_in, cached, prediction, student, wg, wu, wd):
     tok, width = hidden_in.shape
     window = prediction.shape[1]
     nx, ny, nz = lax.axis_size("seq"), NY, lax.axis_size("expert") // NY
     rows = width // nx
     hidden_units = wg.shape[1]
-    arrived = outgoing.shape[0]
+    arrived = router.shape[0] * SLOTS
     chunks = width // CHUNK
     vmem = pl.BlockSpec(memory_space=pltpu.VMEM)
     hbm = pl.BlockSpec(memory_space=pl.ANY)
@@ -445,39 +620,44 @@
             jax.ShapeDtypeStruct((tok, width), BF16),
             jax.ShapeDtypeStruct((rows // (2 * ny * nz), window), F32),
         ),
-        in_specs=[vmem] * 6 + [hbm] * 3,
+        in_specs=[vmem] * 7 + [hbm] * 3,
         out_specs=(vmem, vmem),
         scratch_shapes=[
             pltpu.VMEM((width, hidden_units), BF16),
             pltpu.VMEM((width, hidden_units), BF16),
             pltpu.VMEM((hidden_units, width), BF16),
+            pltpu.VMEM((arrived, tok), BF16),
+            pltpu.VMEM((2 * tok, arrived), BF16),
+            pltpu.VMEM((nz, tok, width), BF16),
+            pltpu.VMEM((nz, arrived // nz, tok), BF16),
             pltpu.VMEM((arrived, width), BF16),
+            pltpu.VMEM((arrived, hidden_units), F32),
+            pltpu.VMEM((arrived, hidden_units), F32),
             pltpu.VMEM((arrived, hidden_units), BF16),
-            pltpu.VMEM((chunks, arrived, CHUNK), BF16),
-            pltpu.VMEM((chunks, arrived, CHUNK), BF16),
+            pltpu.VMEM((arrived, width), BF16),
+            pltpu.VMEM((arrived, width), BF16),
             pltpu.VMEM((tok, width), F32),
-            pltpu.VMEM((5, *early), F32),
-            pltpu.VMEM((1, *early), F32),
-            pltpu.VMEM((nx - 1, *early), F32),
+            pltpu.VMEM((4, *early), F32),
+            pltpu.VMEM((2 * nx - 1, *early), F32),
             pltpu.VMEM((ny - 1, *early), F32),
             pltpu.VMEM((nz - 1, *early), F32),
-            pltpu.VMEM((2, 5, *late), F32),
-            pltpu.VMEM((2, 1, *late), F32),
-            pltpu.VMEM((2, nx - 1, *late), F32),
+            pltpu.VMEM((2, 4, *late), F32),
+            pltpu.VMEM((2, 2 * nx - 1, *late), F32),
             pltpu.VMEM((2, ny - 1, *late), F32),
             pltpu.VMEM((2, nz - 1, *late), F32),
             pltpu.VMEM((nx, rows, tok), BF16),
             pltpu.VMEM((nx, tok, window), BF16),
-            pltpu.VMEM((rows, window), F32),
             pltpu.VMEM((rows // 2, window), F32),
             pltpu.VMEM((ny, rows // (2 * ny), window), F32),
             pltpu.VMEM((nz, rows // (2 * ny * nz), window), F32),
             dma((3,)),
-            dma((4, 2, 6)),
+            dma((2 + chunks, 2, 6)),
+            dma((2, 2, nz - 1)),
+            dma((2, nz - 1)),
             dma((2,)),
             dma((2, chunks)),
             dma((2, nx - 1)),
-            dma((3, 4, 2, 7)),
+            dma((3, 3, 2, 7)),
             dma((2, nx - 1)),
             dma((2, 1)),
             dma((2, ny - 1)),
@@ -486,7 +666,7 @@
         compiler_params=pltpu.CompilerParams(
             collective_id=1, has_side_effects=True, vmem_limit_bytes=60 * 2**20
         ),
-    )(outgoing, mix, hidden_in, cached, prediction, student, wg, wu, wd)
+    )(gain, router, routes, hidden_in, cached, prediction, student, wg, wu, wd)
 
 
 def body(
@@ -502,32 +682,8 @@
     prediction,
 ):
     tok, width = hidden_in.shape
-    n_experts = router_weight.shape[1]
     nx, nz = lax.axis_size("seq"), lax.axis_size("expert") // NY
     total_tokens = tok * lax.axis_size(("expert", "seq", "dp"))
-    hidden32 = hidden_in.astype(F32)
-    normed = (
-        hidden32
-        * lax.rsqrt(jnp.mean(hidden32 * hidden32, axis=-1, keepdims=True) + 1e-06)
-        * norm_gain
-    ).astype(BF16)
-    logits = jnp.dot(normed, router_weight, preferred_element_type=F32)
-    picked = jnp.any(routes[:, :, None] == jnp.arange(n_experts, dtype=jnp.int32), axis=1)
-    earlier = jnp.tril(jnp.ones((tok, tok), BF16), -1)
-    place = jnp.dot(earlier, picked.astype(BF16), preferred_element_type=F32)
-    affinity = jnp.where(picked, jax.nn.sigmoid(logits), 0.0)
-    share = affinity / jnp.sum(affinity, axis=-1, keepdims=True)
-    slots = jnp.arange(SLOTS, dtype=F32)
-    where = picked[:, :, None] & (place[:, :, None] == slots)
-    pick = where.reshape(tok, n_experts * SLOTS).astype(BF16)
-    mix = jnp.where(where, share[:, :, None], 0.0).reshape(tok, n_experts * SLOTS)
-    high = mix.astype(BF16)
-    low = (mix - high.astype(F32)).astype(BF16)
-    mix = jnp.concatenate([high, low], axis=0)
-    outgoing = lax.dot_general(
-        pick, normed, (((0,), (0,)), ((), ())), preferred_element_type=F32
-    ).astype(BF16)
-
     student = (
         student_hidden.T.reshape(nz, NY, nx, 2, width // (2 * nx * NY * nz), tok)
         .transpose(2, 3, 1, 0, 4, 5)
@@ -535,8 +691,9 @@
     )
     return run(
         total_tokens,
-        outgoing,
-        mix,
+        norm_gain[None],
+        router_weight.T,
+        routes.T,
         hidden_in,
         cached_layers,
         prediction,

time: 337 us -> 310 us (0.920)
  Pallas kernels: 321 us -> 303 us
  matrix products: 4.92 us -> 0 us
    pallas_call x1, Pallas kernels: 321 us -> 303 us  [run(): pl.pallas_call(functools.partial(kernel, total_tokens), out_shape=(jax.Sh...]
    dot_general x3 -> x0, matrix products: 4.92 us -> none  [the longest x1 3.27 us: body(): lax.dot_general(pick, normed, (((0,), (0,)), ((), ())), preferred_element...]
where the time goes in v3:
time: 310 us; the launch traced here: 309 us
  Pallas kernels  303 us (98%)
  local copies, waits for them, and re-layouts  5.51 us (2%)
    pallas_call x1, Pallas kernels, run(): pl.pallas_call(functools.partial(kernel, total_tokens), out_shape=(jax.Sh...  303 us

profile of v3, /device:TPU:1, one launch (start us, length us, event | category | flops | bytes accessed | tf_op | source)
XLA Modules:
  0.0 309.3 jit_solution(17548280134192537496)
XLA Ops:
  0.6 1.3 copy.13
  1.9 0.9 copy.14
  2.9 303.1 %shard_map.113 = (bf16[128,2048]{1,0:T(8,128)(2,1)}, f32[8,1024]{1,0:T(8,128)}) custom-call(f32[1,2048]{1,0:T(1,128)} %bitcast.18, bf16[64,2048]{1,0:T(8,128)(2,1)} %bitcast.17, s32[6,128]{1,0:T(8,128)} %bitcast.19, bf16[128,2048]{1,0:T(8,128)(2,1)} %hidden_ref.1, bf16[3,128,2048]{2,1,0:T(8,128)(2,1)} %cached_ref.1, bf16[128,1024]{1,0:T(8,128)(2,1)} %prediction_ref.1, ...), custom_call_target="tpu_custom_call" | custom-call | tf_op jit(solution)/shard_map/pallas_call | solution.py:617
  306.0 1.9 copy.17
  307.9 1.4 copy.18

commit v4 on v3

--- a/solution.py
+++ b/solution.py
@@ -70,6 +70,7 @@
 
 SLOTS = 16
 CHUNK = 512
+STRIDE = 27
 TILE = 256
 
 
@@ -259,9 +260,9 @@
     def block(p):
         return pl.ds(pl.multiple_of(p * SLOTS, SLOTS), SLOTS)
 
-    def scatter(source, target, cols, send, recv):
-        def go(d, _):
-            p, device = peer(d)
+    def scatter(source, target, cols, send, recv, first, end):
+        def go(i, _):
+            p, device = peer(lax.rem(i * STRIDE, n))
             pltpu.make_async_remote_copy(
                 src_ref=source.at[block(p), cols],
                 dst_ref=target.at[block(me), cols],
@@ -272,8 +273,9 @@
             ).start()
             return _
 
-        lax.fori_loop(1, n, go, 0)
-        target[block(me), cols] = source[block(me), cols]
+        lax.fori_loop(first, end, go, 0)
+        if first == 1:
+            target[block(me), cols] = source[block(me), cols]
 
     def wait_rows(ref, count, cols, sem):
         rows = ref.at[pl.ds(0, count * SLOTS), cols]
@@ -370,6 +372,7 @@
                 sem_s.at[number, i, 0],
                 sem_s.at[number, i, 1],
             )
+            yield
             wait_all(copies)
             total = own[i]
             for d in range(1, axes[name][1]):
@@ -384,29 +387,31 @@
     for copy in picks_out:
         copy.wait_recv()
     select(z)
-    for m in range(2):
-        next_ring(m)
+    next_ring(0)
+    next_ring(1)
     select(lax.rem(z + nz - 1, nz))
     select(lax.rem(z + 1, nz))
-    for m in range(2, 4):
-        next_ring(m)
+    pass_on(gate_piece)
+    next_ring(2)
+    next_ring(3)
     select(lax.rem(z + nz - 2, nz))
     select(lax.rem(z + 2, nz))
-    pass_on(gate_piece)
-    for m in range(4, 6):
-        next_ring(m)
-    select(lax.rem(z + nz - 3, nz))
-    select(lax.rem(z + 3, nz))
+    next_ring(4)
+    next_ring(5)
     gate_piece[1].wait_recv()
     gate_piece[3].wait_recv()
     begin(up_piece)
+    select(lax.rem(z + nz - 3, nz))
+    select(lax.rem(z + 3, nz))
     next_ring(6)
     select(lax.rem(z + nz // 2, nz))
-    add_over_devices(0, cached_own, (cached_w, cached_y, cached_z))
+    cached_sums = add_over_devices(0, cached_own, (cached_w, cached_y, cached_z))
+    next(cached_sums, None)
     for copy in mine:
         copy.wait()
     gate_piece[4].wait_recv()
     gate_piece[5].wait_recv()
+    pass_on(up_piece)
     everything = slice(0, width)
     wait_rows(arrived, n - nz, everything, sem_rows.at[1])
 
@@ -434,46 +439,51 @@
         return _
 
     tiles = arrived.shape[0] // TILE
-    lax.fori_loop(0, tiles // 2, gate_tile, 0)
-    pass_on(up_piece)
-    lax.fori_loop(tiles // 2, tiles, gate_tile, 0)
+    next(cached_sums, None)
+    lax.fori_loop(0, tiles, gate_tile, 0)
+    next(cached_sums, None)
     up_piece[1].wait_recv()
     up_piece[3].wait_recv()
     begin(down_pieces[0])
     lax.fori_loop(0, tiles, up_tile, 0)
+    next(cached_sums, None)
     up_piece[4].wait_recv()
     up_piece[5].wait_recv()
     begin(down_pieces[1])
     lax.fori_loop(0, tiles, act_tile, 0)
     wait_rows(out, n - nz, everything, sem_rows.at[0])
-    pass_on(down_pieces[0])
-
-    def send_back(j):
-        cols = slice(j * CHUNK, (j + 1) * CHUNK)
-        scatter(out, back, cols, sem_back.at[0, j], sem_back.at[1, j])
-
-    for j in range(chunks):
-        if j + 2 < chunks:
-            begin(down_pieces[j + 2])
+
+    def columns_of(j):
+        return slice(j * CHUNK, (j + 1) * CHUNK)
+
+    def send_back(j, first, end):
+        scatter(out, back, columns_of(j), sem_back.at[0, j], sem_back.at[1, j], first, end)
+
+    def project(j):
         for i in (1, 3, 4, 5):
             down_pieces[j][i].wait_recv()
-        cols = slice(j * CHUNK, (j + 1) * CHUNK)
-
-        def project(i, _):
+        cols = columns_of(j)
+
+        def project_tile(i, _):
             at = pl.ds(pl.multiple_of(i * TILE, TILE), TILE)
             out[at, cols] = jnp.dot(act[at, :], wd[:, cols], preferred_element_type=F32).astype(BF16)
             return _
 
-        lax.fori_loop(0, tiles, project, 0)
-        if j < chunks // 2:
-            send_back(j)
-        if j + 1 < chunks:
-            pass_on(down_pieces[j + 1])
-
-    for j in range(chunks // 2):
-        wait_rows(out, n - 1, slice(j * CHUNK, (j + 1) * CHUNK), sem_back.at[0, j])
-    for j in range(chunks // 2, chunks):
-        send_back(j)
+        lax.fori_loop(0, tiles, project_tile, 0)
+
+    pass_on(down_pieces[0])
+    begin(down_pieces[2])
+    project(0)
+    pass_on(down_pieces[1])
+    begin(down_pieces[3])
+    send_back(0, 1, n)
+    project(1)
+    pass_on(down_pieces[2])
+    send_back(1, 1, n)
+    project(2)
+    pass_on(down_pieces[3])
+    for j in range(2):
+        wait_rows(out, n - 1, columns_of(j), sem_back.at[0, j])
     scale = 1.0 / math.sqrt(total_tokens)
     tail_cut = 4
 
@@ -487,7 +497,7 @@
 
     def add_statistics(h):
         slots = [s.at[h] for s in (stat_w, stat_y, stat_z)]
-        add_over_devices(1 + h, stat_own.at[h], slots)
+        return add_over_devices(1 + h, stat_own.at[h], slots)
 
     def write_targets(h):
         last = stat_own[h, 3]
@@ -517,81 +527,109 @@
                 ).astype(BF16)
 
     combine(0)
-    add_statistics(0)
+    sums = add_statistics(0)
+    quarter = n // 4
+    next(sums, None)
+    send_back(2, 1, quarter)
+    next(sums, None)
+    send_back(2, quarter, 2 * quarter)
+    next(sums, None)
+    send_back(2, 2 * quarter, 3 * quarter)
+    next(sums, None)
     write_targets(0)
-    copies = start_all(
-        axes["x"],
-        lambda d: residuals.at[0],
-        lambda d: residuals.at[d],
-        sem_x.at[0],
-        sem_x.at[1],
-    )
+    pieces = [slice(k * CHUNK, (k + 1) * CHUNK) for k in range(window // CHUNK)]
+    over_x = [
+        start_all(
+            axes["x"],
+            lambda d: residuals.at[0, :, cols],
+            lambda d: residuals.at[d, :, cols],
+            sem_x.at[k, 0],
+            sem_x.at[k, 1],
+        )
+        for k, cols in enumerate(pieces)
+    ]
+    send_back(2, 3 * quarter, n)
+    project(3)
     wait_all(students_out)
     rows = students.shape[1]
     partial = raised.at[pl.ds(0, rows), pl.ds(0, window)]
     halved = rows // 2
-    for d in range(nx):
-        if d:
-            copies[d - 1].wait_recv()
-
-        def add(i, _):
-            at = pl.ds(pl.multiple_of(i * 128, 128), 128)
-            product = jnp.dot(students[d, at, :], residuals[d], preferred_element_type=F32)
-            partial[at, :] = product if d == 0 else partial[at, :] + product
-            return _
-
-        lax.fori_loop(0, rows // 128, add, 0)
-    for copy in copies:
-        copy.wait_send()
     other = pl.ds(pl.multiple_of((1 - c) * halved, halved), halved)
     kept = pl.ds(pl.multiple_of(c * halved, halved), halved)
-    wait_all(
-        start_all(
-            axes["c"],
-            lambda d: partial.at[other],
-            lambda d: from_c,
-            sem_c.at[0],
-            sem_c.at[1],
-        )
-    )
-    from_c[...] = from_c[...] + partial[kept, :]
     part = halved // ny
+    least = part // nz
 
     def y_rows(d):
         return pl.ds(pl.multiple_of(lax.rem(y + d, ny) * part, part), part)
 
-    copies = start_all(
-        axes["y"],
-        lambda d: from_c.at[y_rows(d)],
-        lambda d: from_y.at[d],
-        sem_y.at[0],
-        sem_y.at[1],
-    )
-    combine(1)
-    add_statistics(1)
-    wait_all(copies)
-    total = from_c[y_rows(0), :]
-    for d in range(1, ny):
-        total = total + from_y[d]
-    from_y[0] = total
-    least = part // nz
-
     def z_rows(d):
         return pl.ds(pl.multiple_of(lax.rem(z + d, nz) * least, least), least)
 
-    copies = start_all(
-        axes["z"],
-        lambda d: from_y.at[0, z_rows(d)],
-        lambda d: from_z.at[d],
-        sem_z.at[0],
-        sem_z.at[1],
-    )
+    over_c, over_y, over_z = [], [], []
+    for k, cols in enumerate(pieces):
+        for d in range(nx):
+            if d:
+                over_x[k][d - 1].wait_recv()
+
+            def add(i, _):
+                at = pl.ds(pl.multiple_of(i * 128, 128), 128)
+                product = jnp.dot(
+                    students[d, at, :], residuals[d, :, cols], preferred_element_type=F32
+                )
+                partial[at, cols] = product if d == 0 else partial[at, cols] + product
+                return _
+
+            lax.fori_loop(0, rows // 128, add, 0)
+        over_c.append(
+            start_all(
+                axes["c"],
+                lambda d: partial.at[other, cols],
+                lambda d: from_c.at[:, cols],
+                sem_c.at[k, 0],
+                sem_c.at[k, 1],
+            )
+        )
+        send_back(3, 2 * quarter * k + (k == 0), 2 * quarter * (k + 1))
+    for k, cols in enumerate(pieces):
+        wait_all(over_c[k])
+        from_c[:, cols] = from_c[:, cols] + partial[kept, cols]
+        over_y.append(
+            start_all(
+                axes["y"],
+                lambda d: from_c.at[y_rows(d), cols],
+                lambda d: from_y.at[d, :, cols],
+                sem_y.at[k, 0],
+                sem_y.at[k, 1],
+            )
+        )
+    for k, cols in enumerate(pieces):
+        wait_all(over_y[k])
+        total = from_c[y_rows(0), cols]
+        for d in range(1, ny):
+            total = total + from_y[d, :, cols]
+        from_y[0, :, cols] = total
+        over_z.append(
+            start_all(
+                axes["z"],
+                lambda d: from_y.at[0, z_rows(d), cols],
+                lambda d: from_z.at[d, :, cols],
+                sem_z.at[k, 0],
+                sem_z.at[k, 1],
+            )
+        )
+    combine(1)
+    sums = add_statistics(1)
+    for _ in range(4):
+        next(sums, None)
     write_targets(1)
-    wait_all(copies)
-    total = from_y[0, z_rows(0), :]
-    for d in range(1, nz):
-        total = total + from_z[d]
-    grad_ref[...] = total
+    for k, cols in enumerate(pieces):
+        wait_all(over_z[k])
+        total = from_y[0, z_rows(0), cols]
+        for d in range(1, nz):
+            total = total + from_z[d, :, cols]
+        grad_ref[:, cols] = total
+        for copy in over_x[k]:
+            copy.wait_send()
 
     for piece in (gate_piece, up_piece, *down_pieces):
         for copy in piece:
@@ -608,6 +646,7 @@
     nx, ny, nz = lax.axis_size("seq"), NY, lax.axis_size("expert") // NY
     rows = width // nx
     hidden_units = wg.shape[1]
+    pieces = window // CHUNK
     arrived = router.shape[0] * SLOTS
     chunks = width // CHUNK
     vmem = pl.BlockSpec(memory_space=pltpu.VMEM)
@@ -658,10 +697,10 @@
             dma((2, chunks)),
             dma((2, nx - 1)),
             dma((3, 3, 2, 7)),
-            dma((2, nx - 1)),
-            dma((2, 1)),
-            dma((2, ny - 1)),
-            dma((2, nz - 1)),
+            dma((pieces, 2, nx - 1)),
+            dma((pieces, 2, 1)),
+            dma((pieces, 2, ny - 1)),
+            dma((pieces, 2, nz - 1)),
         ],
         compiler_params=pltpu.CompilerParams(
             collective_id=1, has_side_effects=True, vmem_limit_bytes=60 * 2**20

time: 310 us -> 266 us (0.86)
  Pallas kernels: 303 us -> 259 us
    pallas_call x1, Pallas kernels: 303 us -> 259 us  [run(): pl.pallas_call(functools.partial(kernel, total_tokens), out_shape=(jax.Sh...]
where the time goes in v4:
time: 266 us
  Pallas kernels  259 us (97%)
  local copies, waits for them, and re-layouts  5.51 us (2%)
    pallas_call x1, Pallas kernels, run(): pl.pallas_call(functools.partial(kernel, total_tokens), out_shape=(jax.Sh...  259 us

profile of v4, /device:TPU:1, one launch (start us, length us, event | category | flops | bytes accessed | tf_op | source)
XLA Modules:
  0.0 265.5 jit_solution(17297726587805963609)
XLA Ops:
  0.6 1.3 copy.13
  1.9 0.9 copy.14
  2.9 259.3 %shard_map.113 = (bf16[128,2048]{1,0:T(8,128)(2,1)}, f32[8,1024]{1,0:T(8,128)}) custom-call(f32[1,2048]{1,0:T(1,128)} %bitcast.18, bf16[64,2048]{1,0:T(8,128)(2,1)} %bitcast.17, s32[6,128]{1,0:T(8,128)} %bitcast.19, bf16[128,2048]{1,0:T(8,128)(2,1)} %hidden_ref.1, bf16[3,128,2048]{2,1,0:T(8,128)(2,1)} %cached_ref.1, bf16[128,1024]{1,0:T(8,128)(2,1)} %prediction_ref.1, ...), custom_call_target="tpu_custom_call" | custom-call | tf_op jit(solution)/shard_map/pallas_call | solution.py:656
  262.2 1.9 copy.17
  264.1 1.4 copy.18

commit v5 on v4

--- a/solution.py
+++ b/solution.py
@@ -127,8 +127,8 @@
     router_ref,
     routes_ref,
     hidden_ref,
-    cached_ref,
-    prediction_ref,
+    cached_in,
+    prediction_in,
     student_ref,
     wg_ref,
     wu_ref,
@@ -138,6 +138,8 @@
     wg,
     wu,
     wd,
+    cached_ref,
+    prediction_ref,
     pick_ref,
     mix_ref,
     blocks,
@@ -199,6 +201,19 @@
     lax.fori_loop(1, n, greet, 0)
     for d in range(1, 2 * nx):
         pl.semaphore_signal(barrier, inc=1, device_id=axes["w"][2](d), device_id_type=MESH)
+    mine = []
+
+    def bring(source, target):
+        copy = pltpu.make_async_copy(source, target, sem_own.at[len(mine)])
+        copy.start()
+        mine.append(copy)
+
+    bring(cached_in, cached_ref)
+    bring(prediction_in, prediction_ref)
+    bring(student_ref.at[x], students.at[0])
+    for shard, whole in ((wg_ref, wg), (wu_ref, wu), (wd_ref, wd)):
+        rows = shard.shape[0]
+        bring(shard, whole.at[pl.ds(pl.multiple_of(x * rows, 16), rows)])
     pl.semaphore_wait(barrier, n - 1 + 2 * nx - 1)
 
     right, left = axes["x"][2](1), axes["x"][2](nx - 1)
@@ -346,14 +361,6 @@
     start_ring(0)
     start_ring(1)
     picks[z] = pick_ref[group_rows(z), :]
-    mine = []
-    for i, (shard, whole) in enumerate(((wg_ref, wg), (wu_ref, wu), (wd_ref, wd))):
-        rows = shard.shape[0]
-        copy = pltpu.make_async_copy(
-            shard, whole.at[pl.ds(pl.multiple_of(x * rows, 16), rows)], sem_own.at[i]
-        )
-        copy.start()
-        mine.append(copy)
     students_out = start_all(
         axes["x"],
         lambda d: student_ref.at[lax.rem(x + d, nx)],
@@ -361,7 +368,6 @@
         sem_st.at[0],
         sem_st.at[1],
     )
-    students[0] = student_ref[x]
 
     def add_over_devices(number, own, slots):
         for i, name in enumerate("wyz"):
@@ -379,6 +385,7 @@
                 total = total + slots[i][d - 1]
             own[i + 1] = total
 
+    mine[0].wait()
     stats = []
     for layer in range(3):
         stats += column_sums(cached_ref[layer].astype(F32))
@@ -407,7 +414,7 @@
     select(lax.rem(z + nz // 2, nz))
     cached_sums = add_over_devices(0, cached_own, (cached_w, cached_y, cached_z))
     next(cached_sums, None)
-    for copy in mine:
+    for copy in mine[1:]:
         copy.wait()
     gate_piece[4].wait_recv()
     gate_piece[5].wait_recv()
@@ -526,15 +533,15 @@
                     (prediction_ref[:, cols].astype(F32) - targets.astype(F32)) * scale
                 ).astype(BF16)
 
+    send_back(2, 1, 20)
     combine(0)
     sums = add_statistics(0)
-    quarter = n // 4
     next(sums, None)
-    send_back(2, 1, quarter)
+    send_back(2, 20, 28)
     next(sums, None)
-    send_back(2, quarter, 2 * quarter)
+    send_back(2, 28, 36)
     next(sums, None)
-    send_back(2, 2 * quarter, 3 * quarter)
+    send_back(2, 36, 44)
     next(sums, None)
     write_targets(0)
     pieces = [slice(k * CHUNK, (k + 1) * CHUNK) for k in range(window // CHUNK)]
@@ -548,8 +555,9 @@
         )
         for k, cols in enumerate(pieces)
     ]
-    send_back(2, 3 * quarter, n)
+    send_back(2, 44, n)
     project(3)
+    send_back(3, 1, 20)
     wait_all(students_out)
     rows = students.shape[1]
     partial = raised.at[pl.ds(0, rows), pl.ds(0, window)]
@@ -589,7 +597,7 @@
                 sem_c.at[k, 1],
             )
         )
-        send_back(3, 2 * quarter * k + (k == 0), 2 * quarter * (k + 1))
+        send_back(3, (20, 42)[k], (42, n)[k])
     for k, cols in enumerate(pieces):
         wait_all(over_c[k])
         from_c[:, cols] = from_c[:, cols] + partial[kept, cols]
@@ -659,12 +667,14 @@
             jax.ShapeDtypeStruct((tok, width), BF16),
             jax.ShapeDtypeStruct((rows // (2 * ny * nz), window), F32),
         ),
-        in_specs=[vmem] * 7 + [hbm] * 3,
+        in_specs=[vmem] * 4 + [hbm] * 6,
         out_specs=(vmem, vmem),
         scratch_shapes=[
             pltpu.VMEM((width, hidden_units), BF16),
             pltpu.VMEM((width, hidden_units), BF16),
             pltpu.VMEM((hidden_units, width), BF16),
+            pltpu.VMEM(cached.shape, BF16),
+            pltpu.VMEM(prediction.shape, BF16),
             pltpu.VMEM((arrived, tok), BF16),
             pltpu.VMEM((2 * tok, arrived), BF16),
             pltpu.VMEM((nz, tok, width), BF16),
@@ -689,7 +699,7 @@
             pltpu.VMEM((rows // 2, window), F32),
             pltpu.VMEM((ny, rows // (2 * ny), window), F32),
             pltpu.VMEM((nz, rows // (2 * ny * nz), window), F32),
-            dma((3,)),
+            dma((6,)),
             dma((2 + chunks, 2, 6)),
             dma((2, 2, nz - 1)),
             dma((2, nz - 1)),

time: 266 us -> 260 us (0.977)
  Pallas kernels: 259 us -> 254 us
    pallas_call x1, Pallas kernels: 259 us -> 254 us  [run(): pl.pallas_call(functools.partial(kernel, total_tokens), out_shape=(jax.Sh...]
where the time goes in v5:
time: 260 us
  Pallas kernels  254 us (98%)
  local copies, waits for them, and re-layouts  5.51 us (2%)
    pallas_call x1, Pallas kernels, run(): pl.pallas_call(functools.partial(kernel, total_tokens), out_shape=(jax.Sh...  254 us

profile of v5, /device:TPU:1, one launch (start us, length us, event | category | flops | bytes accessed | tf_op | source)
XLA Modules:
  0.0 260.2 jit_solution(16406588187688013950)
XLA Ops:
  0.6 1.3 copy.13
  1.9 0.9 copy.14
  2.9 254.1 %shard_map.113 = (bf16[128,2048]{1,0:T(8,128)(2,1)}, f32[8,1024]{1,0:T(8,128)}) custom-call(f32[1,2048]{1,0:T(1,128)} %bitcast.18, bf16[64,2048]{1,0:T(8,128)(2,1)} %bitcast.17, s32[6,128]{1,0:T(8,128)} %bitcast.19, bf16[128,2048]{1,0:T(8,128)(2,1)} %hidden_ref.1, bf16[3,128,2048]{2,1,0:T(8,128)(2,1)} %cached_in.1, bf16[128,1024]{1,0:T(8,128)(2,1)} %prediction_in.1, ...), custom_call_target="tpu_custom_call" | custom-call | tf_op jit(solution)/shard_map/pallas_call | solution.py:664
  257.0 1.9 copy.17
  258.8 1.4 copy.18

commit v6 on v5

--- a/solution.py
+++ b/solution.py
@@ -485,8 +485,8 @@
     begin(down_pieces[3])
     send_back(0, 1, n)
     project(1)
+    send_back(1, 1, n)
     pass_on(down_pieces[2])
-    send_back(1, 1, n)
     project(2)
     pass_on(down_pieces[3])
     for j in range(2):

time: 260 us -> 260 us (level)
  no operation moved by 1% of the time
where the time goes in v6:
time: 260 us
  Pallas kernels  254 us (98%)
  local copies, waits for them, and re-layouts  5.51 us (2%)
    pallas_call x1, Pallas kernels, run(): pl.pallas_call(functools.partial(kernel, total_tokens), out_shape=(jax.Sh...  254 us

profile of v6, /device:TPU:1, one launch (start us, length us, event | category | flops | bytes accessed | tf_op | source)
XLA Modules:
  0.0 260.2 jit_solution(1952090823085391896)
XLA Ops:
  0.6 1.3 copy.13
  1.9 0.9 copy.14
  2.9 254.1 %shard_map.113 = (bf16[128,2048]{1,0:T(8,128)(2,1)}, f32[8,1024]{1,0:T(8,128)}) custom-call(f32[1,2048]{1,0:T(1,128)} %bitcast.18, bf16[64,2048]{1,0:T(8,128)(2,1)} %bitcast.17, s32[6,128]{1,0:T(8,128)} %bitcast.19, bf16[128,2048]{1,0:T(8,128)(2,1)} %hidden_ref.1, bf16[3,128,2048]{2,1,0:T(8,128)(2,1)} %cached_in.1, bf16[128,1024]{1,0:T(8,128)(2,1)} %prediction_in.1, ...), custom_call_target="tpu_custom_call" | custom-call | tf_op jit(solution)/shard_map/pallas_call | solution.py:664
  257.0 1.9 copy.17
  258.8 1.4 copy.18
